TPU v7x, 256 devices: a whole 4x4x8 slice. The times are simulated.
256 devices in a mesh: dp: 128 (over z, y_hi, x, core), mp: 2 (over y_lo).
Axes of the slice: x: 4, y: 4 (y_hi: 2, y_lo: 2; y = y_hi * 2 + y_lo), z: 8, core: 2. Of those that a mesh axis runs over, the one named last changes fastest.
Arguments:
- page_hidden: bfloat16 [256, 1030, 2048], P('dp', 'mp'), may hold values from -24 to 24
- query_hidden: bfloat16 [256, 32, 2048], P('dp', 'mp'), may hold values from -24 to 24
- page_pre: bfloat16 [256, 1030, 128], P('dp')
- query_pre: bfloat16 [256, 32, 128], P('dp')
- match_index: int32 [256, 2, 64], P('dp'), may hold values from 0 to 1029, as said below
- positive: int32 [256], P('dp'), may hold values from 0 to 255, as said below
Outputs:
- d_page_pre: float32 [256, 1030, 128], P('dp', 'mp')
- d_query_pre: float32 [256, 32, 128], P('dp', 'mp')
- grad_weight: float32 [2048, 128], P(('dp', 'mp'))
Inputs may be any that keep to these rules, and one draw needn't show every extreme that they name: match_index[c, v, i * 32 + t]: the patch of page c matched to token t of query i of block (c // 2 - v) mod (128). positive[q] lies in block q // 2 or the next block around the cycle.
All inputs are finite; a program needn't handle non-finite values.
Results may differ from a plain program's by a relative error of at most 0.009.
Values may be sent and summed in bfloat16 or wider, within the bound.
No kernel may reach another device: no remote copies, remote signals or barrier semaphores. Data moves between devices by JAX's collectives and lax.ppermute only.
A program may use at most 64 MiB of HBM per device.

v0:
```python
import jax
import jax.numpy as jnp
from jax import lax
from jax.sharding import PartitionSpec as P

SCALE_LOGIT = 10.0
EPS = 1e-06


def shifted(block, axis, distance):
    devices = range(lax.axis_size(axis))
    route = [((i - distance) % len(devices), i) for i in devices]
    return lax.ppermute(block, axis, route)


def token_scores(queries, gathered, per_dev, qtokens):
    prods = jnp.sum(gathered.astype(jnp.float32) * queries.astype(jnp.float32)[None], axis=-1)
    return jnp.sum(prods.reshape(per_dev, per_dev, qtokens), axis=-1).T


def query_grads(weights, gathered, per_dev, qtokens):
    rows_wide = gathered.astype(jnp.float32).reshape(per_dev, per_dev, qtokens, -1)
    return SCALE_LOGIT * jnp.einsum("ic,cite->ite", weights, rows_wide)


def row_values(weights, queries, per_dev, qtokens):
    query_wide = queries.astype(jnp.float32).reshape(per_dev, qtokens, -1)
    return SCALE_LOGIT * jnp.einsum("ic,ite->cite", weights, query_wide).reshape(
        per_dev, per_dev * qtokens, -1
    )


def patch_grads(where, values, patch_count, patch_start):

    def single(spots, vals):
        rows_here = lax.broadcasted_iota(jnp.int32, (patch_count, spots.shape[0]), 0) + patch_start
        table = (rows_here == spots[None, :]).astype(jnp.float32)
        return jnp.dot(
            table, vals, precision=lax.Precision.HIGHEST, preferred_element_type=jnp.float32
        )

    return jax.vmap(single)(where, values)


def contract_rows(left, right):
    return lax.dot_general(
        left, right, (((0,), (0,)), ((), ())), preferred_element_type=jnp.float32
    )


def shards(page_hidden, query_hidden, page_pre, query_pre, match_index, positive):
    per_dev = page_pre.shape[0]
    qtokens = query_pre.shape[1]
    width = page_pre.shape[2]
    patch_count = page_hidden.shape[1]
    token_count = query_hidden.shape[1]
    cycle_size = lax.axis_size("dp")
    cycle_index = lax.axis_index("dp")
    split_index = lax.axis_index("mp")
    patch_start = split_index * patch_count
    token_start = split_index * token_count
    page_wide = page_pre.astype(jnp.float32)
    query_wide = query_pre.astype(jnp.float32)
    norm_p = jnp.sqrt(jnp.sum(page_wide * page_wide, axis=-1, keepdims=True) + EPS)
    norm_q = jnp.sqrt(jnp.sum(query_wide * query_wide, axis=-1, keepdims=True) + EPS)
    unit_p = page_wide / norm_p
    unit_q = query_wide / norm_q
    emb_p = unit_p.astype(jnp.bfloat16)
    own_queries = unit_q.astype(jnp.bfloat16).reshape(per_dev * qtokens, width)
    gathered = jax.vmap(lambda table, spots: table[spots])(emb_p, match_index)
    own_rows = gathered[:, 0]
    prev_queries = shifted(own_queries, "dp", 1)
    other_scores = token_scores(prev_queries, gathered[:, 1], per_dev, qtokens)
    next_scores = shifted(other_scores, "dp", -1)
    own_scores = token_scores(own_queries, own_rows, per_dev, qtokens)
    logits = SCALE_LOGIT * jnp.concatenate([own_scores, next_scores], axis=-1)
    column = (
        positive // per_dev - cycle_index + cycle_size
    ) % cycle_size * per_dev + positive % per_dev
    onehot = (column[:, None] == jnp.arange(2 * per_dev, dtype=jnp.int32)[None, :]).astype(
        jnp.float32
    )
    grads = (jax.nn.softmax(logits, axis=-1) - onehot) / (per_dev * cycle_size)
    grad_own = grads[:, :per_dev]
    grad_next = grads[:, per_dev:]
    values_own = row_values(grad_own, own_queries, per_dev, qtokens)
    d_query = query_grads(grad_own, own_rows, per_dev, qtokens)
    grad_prev = shifted(grad_next, "dp", 1)
    partial_prev = query_grads(grad_prev, gathered[:, 1], per_dev, qtokens)
    d_query = d_query + shifted(partial_prev, "dp", -1)
    values_prev = row_values(grad_prev, prev_queries, per_dev, qtokens)
    values = jnp.stack([values_own, values_prev], axis=1).reshape(
        per_dev, 2 * per_dev * qtokens, width
    )
    d_page = patch_grads(match_index.reshape(per_dev, -1), values, patch_count, patch_start)
    unit_ph = lax.dynamic_slice_in_dim(unit_p, patch_start, patch_count, 1)
    norm_ph = lax.dynamic_slice_in_dim(norm_p, patch_start, patch_count, 1)
    d_query_h = lax.dynamic_slice_in_dim(d_query, token_start, token_count, 1)
    unit_qh = lax.dynamic_slice_in_dim(unit_q, token_start, token_count, 1)
    norm_qh = lax.dynamic_slice_in_dim(norm_q, token_start, token_count, 1)
    d_page_pre = (d_page - unit_ph * jnp.sum(unit_ph * d_page, axis=-1, keepdims=True)) / norm_ph
    d_query_pre = (
        d_query_h - unit_qh * jnp.sum(unit_qh * d_query_h, axis=-1, keepdims=True)
    ) / norm_qh
    low_p = d_page_pre.astype(jnp.bfloat16).reshape(-1, width)
    low_q = d_query_pre.astype(jnp.bfloat16).reshape(-1, width)
    share = page_hidden.shape[2] // (cycle_size * lax.axis_size("mp"))
    slab_p = page_hidden.reshape(-1, lax.axis_size(("dp", "mp")) * share)
    slab_q = query_hidden.reshape(-1, lax.axis_size(("dp", "mp")) * share)
    grad_weight = lax.psum_scatter(
        contract_rows(slab_p, low_p) + contract_rows(slab_q, low_q),
        ("dp", "mp"),
        scatter_dimension=0,
        tiled=True,
    )
    return (d_page_pre, d_query_pre, grad_weight)


def solution(mesh):
    placed = (
        P("dp", "mp", None),
        P("dp", "mp", None),
        P("dp", None, None),
        P("dp", None, None),
        P("dp", None, None),
        P("dp"),
    )
    return jax.shard_map(
        shards,
        mesh=mesh,
        in_specs=placed,
        out_specs=(P("dp", "mp", None), P("dp", "mp", None), P(("dp", "mp"), None)),
        check_vma=False,
    )
```

profile of v0, /device:TPU:32, one launch (start us, length us, event | category | flops | bytes accessed | tf_op | source)
XLA Modules:
  0.0 305.9 jit_solution(9080441621129167727)
XLA Ops:
  7.2 0.8 fusion.25
  8.1 0.8 fusion.57
  8.9 0.1 collective-permute-start
  9.0 1.4 fusion.15
  10.4 1.4 convert_divide_fusion
  11.9 3.8 %copy.15 = bf16[2,1030,128]{2,0,1:T(2,128)(2,1)S(1)} copy(bf16[2,1030,128]{2,1,0:T(8,128)(2,1)S(1)} %get-tuple-element.14) | data formatting | bytes 1054720 | tf_op jit(solution)/shard_map/convert_element_type | solution.py:68
  15.7 0.1 reshape.123
  15.9 1.4 gather_fusion
  17.4 0.1 eq.32
  17.5 0.1 fusion.24
  17.6 0.1 reshape.115
  17.7 0.1 reduce_sum.86
  17.8 6.2 %collective-permute-start.1 = (f32[2,2]{0,1:T(2,128)S(1)}, f32[2,2]{0,1:T(2,128)S(1)}, u32[]{:S(2)}, u32[]{:S(2)}) collective-permute-start(f32[2,2]{0,1:T(2,128)S(1)} %bitcast.66), channel_id=1, source_target_pairs={{2,0},{4,2},{6,4},{8,6},{10,8},{12,10},{14,12},{16,14},{18,16},{20... | collective-permute-start | bytes 56 | tf_op jit(solution)/shard_map/ppermute | solution.py:13
  24.1 0.1 reshape.114
  24.1 0.1 reduce_sum.84
  24.2 1.1 collective-permute-done.1
  25.5 0.1 collective-permute-start.2
  25.5 0.1 copy.19
  25.7 0.2 fusion.28
  25.9 7.1 %collective-permute-done.2 = f32[2,2]{0,1:T(2,128)S(1)} collective-permute-done((f32[2,2]{0,1:T(2,128)S(1)}, f32[2,2]{0,1:T(2,128)S(1)}, u32[]{:S(2)}, u32[]{:S(2)}) %collective-permute-start.2) | collective-permute-done | bytes 48 | tf_op jit(solution)/shard_map/ppermute | solution.py:13
  33.0 0.1 copy.22
  33.1 0.2 fusion.26
  33.3 0.1 collective-permute-start.3
  33.5 0.6 fusion.16
  34.1 1.9 fusion.11
  36.1 5.0 %fusion.4 = f32[128,2048]{1,0:T(8,128)S(1)} fusion(bf16[2,515,2048]{2,0,1:T(2,128)(2,1)} %param.6, f32[2,515,128]{2,1,0:T(8,128)S(1)} %fusion.11), kind=kOutput, calls=%fused_computation.5 | convolution fusion | flops 540148480 | bytes 5794816 | tf_op jit(solution)/shard_map/dot_general | solution.py:46
  41.0 1.5 fusion.8
  42.6 1.1 copy.17
  43.6 0.7 fusion.14
  44.3 253.1 %all-reduce.3.cloned.1.call-done = f32[2048,128]{0,1:T(8,128)} async-done(((f32[2048,128]{0,1:T(8,128)}), f32[2048,128]{0,1:T(8,128)}) %all-reduce.3.cloned.1.call-update) | async-done | bytes 1048592
  297.5 0.9 constant_dynamic-slice_fusion.2
  298.4 0.7 copy.18
  (29 shorter events, 0.6 us)
Async XLA Ops:
  7.2 33.9 %copy-start = (bf16[2,16,2048]{2,1,0:T(8,128)(2,1)S(1)}, bf16[2,16,2048]{2,1,0:T(8,128)(2,1)}, u32[]{:S(2)}) copy-start(bf16[2,16,2048]{2,1,0:T(8,128)(2,1)} %param.7) | copy-start | bytes 393220
  7.2 290.3 %all-reduce.3.cloned.1.call-start = ((), (), s32[]{:S(2)}) async-start(), calls=%async_computation | async-start | bytes 2097152
  8.9 8.6 %collective-permute-start = (bf16[64,128]{1,0:T(8,128)(2,1)S(1)}, bf16[64,128]{1,0:T(8,128)(2,1)S(1)}, u32[]{:S(2)}, u32[]{:S(2)}) collective-permute-start(bf16[64,128]{1,0:T(8,128)(2,1)S(1)} %bitcast.55), channel_id=1, source_target_pairs={{254,0},{0,2},{2,4},{4,6},{6,8},{8,10},{10,12},{12,14},{14,16},{16... | collective-permute-start | bytes 49160 | tf_op jit(solution)/shard_map/ppermute | solution.py:13
  11.8 3.9 %copy-start.1 = (s32[2,2,64]{2,1,0:T(2,128)S(1)}, s32[2,2,64]{2,1,0:T(2,128)}, u32[]{:S(2)}) copy-start(s32[2,2,64]{2,1,0:T(2,128)} %param.10) | copy-start | bytes 3076
  11.8 5.5 %copy-start.2 = (s32[2]{0:T(128)S(1)}, s32[2]{0:T(128)}, u32[]{:S(2)}) copy-start(s32[2]{0:T(128)} %param.11) | copy-start | bytes 28
  17.8 7.5 %collective-permute-start.1 = (f32[2,2]{0,1:T(2,128)S(1)}, f32[2,2]{0,1:T(2,128)S(1)}, u32[]{:S(2)}, u32[]{:S(2)}) collective-permute-start(f32[2,2]{0,1:T(2,128)S(1)} %bitcast.66), channel_id=1, source_target_pairs={{2,0},{4,2},{6,4},{8,6},{10,8},{12,10},{14,12},{16,14},{18,16},{20... | collective-permute-start | bytes 56 | tf_op jit(solution)/shard_map/ppermute | solution.py:13
  25.5 7.6 %collective-permute-start.2 = (f32[2,2]{0,1:T(2,128)S(1)}, f32[2,2]{0,1:T(2,128)S(1)}, u32[]{:S(2)}, u32[]{:S(2)}) collective-permute-start(f32[2,2]{0,1:T(2,128)S(1)} %get-tuple-element.19), channel_id=1, source_target_pairs={{254,0},{0,2},{2,4},{4,6},{6,8},{8,10},{10,12},{12,14},{14,16},{16... | collective-permute-start | bytes 56 | tf_op jit(solution)/shard_map/ppermute | solution.py:13
  33.3 7.7 %collective-permute-start.3 = (f32[2,32,128]{2,1,0:T(8,128)S(1)}, f32[2,32,128]{2,1,0:T(8,128)S(1)}, u32[]{:S(2)}, u32[]{:S(2)}) collective-permute-start(f32[2,32,128]{2,1,0:T(8,128)S(1)} %broadcast_multiply_fusion), channel_id=1, source_target_pairs={{2,0},{4,2},{6,4},{8,6},{10,8},{12,10},{14,12},{16,14},{18,16},{20... | collective-permute-start | bytes 98312 | tf_op jit(solution)/shard_map/ppermute | solution.py:13
Sparse Core Ops, SparseCore 0:
  42.7 254.7 all-reduce.2
where the time goes:
time: 309 us; the launch traced here: 306 us
  waiting for transfers between devices  261 us (84%)
  between operations  14.2 us (5%)
  local copies, waits for them, and re-layouts  8.62 us (3%)
  other arithmetic  7.71 us (2%)
  matrix products  7.38 us (2%)
  starting transfers between devices  6.53 us (2%)
    unnamed x2, waiting for transfers between devices  253 us
    ppermute x4, waiting for transfers between devices, shifted(): return lax.ppermute(block, axis, route)  8.27 us
    ppermute x4, starting transfers between devices, shifted(): return lax.ppermute(block, axis, route)  6.49 us
    dot_general x2, matrix products, contract_rows(): lax.dot_general(left, right, (((0,), (0,)), ((), ())), preferred_element_...  6.43 us
  transfers between devices with their start and end apart: 5, of which 3 were waited for; matrix products, arithmetic and copies ran while one was open for 6% of the time, Pallas kernels for 0%

commit v1 on v0

v1 whole, which is shorter than its diff:
```python
import functools

import jax
import jax.numpy as jnp
from jax import lax
from jax.experimental import pallas as pl
from jax.experimental.pallas import tpu as pltpu
from jax.sharding import Mesh, PartitionSpec as P

SCALE_LOGIT = 10.0
EPS = 1e-06
F32 = jnp.float32
BF16 = jnp.bfloat16


def slot_row(idx_ref, page):
    return jnp.concatenate([idx_ref[page, 0:1, :], idx_ref[page, 1:2, :]], axis=1)


def inverse_norm(wide):
    return lax.rsqrt(jnp.sum(wide * wide, axis=-1, keepdims=True) + EPS)


def rounded_unit(raw):
    wide = raw.astype(F32)
    return (wide * inverse_norm(wide)).astype(BF16).astype(F32)


def gather_kernel(blocks, pos_ref, idx_ref, page_ref, query_ref, first_ref, second_ref, rows_ref):
    per_dev, patches, width = page_ref.shape
    slots = idx_ref.shape[1] * idx_ref.shape[2]
    half = slots // 2
    own, visiting = [], []
    for page in range(per_dev):
        spots = slot_row(idx_ref, page)
        table = (lax.broadcasted_iota(jnp.int32, (patches, slots), 0) == spots).astype(BF16)
        rows = lax.dot_general(
            table, page_ref[page], (((0,), (0,)), ((), ())), preferred_element_type=F32
        ).astype(BF16)
        rows_ref[pl.ds(page * slots, slots), :] = rows
        own.append(rows[:half])
        visiting.append(rows[half:])
    block = lax.axis_index("blk") * 2 + lax.axis_index("core")
    even = lax.axis_index("core") == 0
    lane = lax.broadcasted_iota(jnp.int32, (16, width), 1)
    meta = jnp.zeros((16, width), F32)
    for i in range(per_dev):
        target = pos_ref[i]
        column = (target // per_dev - block + blocks) % blocks * per_dev + target % per_dev
        meta = jnp.where(lane == i, column.astype(F32), meta)
    own = jnp.concatenate(own, axis=0)
    visiting = jnp.concatenate(visiting, axis=0)
    count = own.shape[0]
    first_ref[0:count, :] = jnp.where(even, own, visiting)
    second_ref[0:count, :] = jnp.where(even, visiting, own)
    queries = query_ref[...].reshape(-1, width)
    tail = jnp.concatenate([queries, meta.astype(BF16)], axis=0)
    first_ref[count:, :] = tail
    second_ref[count:, :] = tail


def loss_grads(unit_q, own_rows, other_rows, columns, per_dev, qtokens, pages):
    grads = []
    for i in range(per_dev):
        query = unit_q[i * qtokens : (i + 1) * qtokens]
        scores = []
        for rows in (own_rows, other_rows):
            for c in range(per_dev):
                start = (c * per_dev + i) * qtokens
                prods = jnp.sum(query * rows[start : start + qtokens], axis=0, keepdims=True)
                scores.append(SCALE_LOGIT * jnp.sum(prods, axis=1, keepdims=True))
        top = functools.reduce(jnp.maximum, scores)
        parts = [jnp.exp(s - top) for s in scores]
        total = functools.reduce(jnp.add, parts)
        grads.append(
            [
                (part / total - (columns[i] == j).astype(F32)) * (SCALE_LOGIT / pages)
                for j, part in enumerate(parts)
            ]
        )
    return grads


def main_kernel(
    pages, pos_ref, idx_ref, first_ref, second_ref, rows_ref, query_ref, half_ref, qhid_ref, hid_ref,
    d_page_ref, d_query_ref, send_ref, keep_ref, hid, sem,
):
    per_dev, patches, width = half_ref.shape
    slots = idx_ref.shape[1] * idx_ref.shape[2]
    half = slots // 2
    qtokens = query_ref.shape[1]
    tokens = qhid_ref.shape[1]
    copies = [pltpu.make_async_copy(hid_ref.at[c], hid.at[c], sem.at[c]) for c in range(per_dev)]
    for copy in copies:
        copy.start()
    blocks = pages // per_dev
    core = lax.axis_index("core")
    split = lax.axis_index("mp")
    block = lax.axis_index("blk") * 2 + core
    even = core == 0
    count = per_dev * half
    qcount = per_dev * qtokens

    first, second = first_ref[...], second_ref[...]
    after = jnp.where(even, first[:count], second[:count])
    before = jnp.where(even, second, first)
    own_unit = rounded_unit(jnp.concatenate([rows_ref[c * slots : c * slots + half] for c in range(per_dev)], axis=0))
    visit_unit = rounded_unit(
        jnp.concatenate([rows_ref[c * slots + half : (c + 1) * slots] for c in range(per_dev)], axis=0)
    )
    after_unit = rounded_unit(after)
    before_rows = rounded_unit(before[:count])
    before_q = rounded_unit(before[count : count + qcount])
    q_wide = query_ref[...].reshape(qcount, width).astype(F32)
    q_inv = inverse_norm(q_wide)
    q_unit = q_wide * q_inv
    q_low = q_unit.astype(BF16).astype(F32)

    columns = []
    for i in range(per_dev):
        target = pos_ref[i]
        columns.append(
            jnp.full((1, 1), (target // per_dev - block + blocks) % blocks * per_dev + target % per_dev).astype(F32)
        )
    meta = before[count + qcount :].astype(F32)
    before_columns = [meta[0:1, i : i + 1] for i in range(per_dev)]
    grads = loss_grads(q_low, own_unit, after_unit, columns, per_dev, qtokens, pages)
    before_grads = loss_grads(before_q, before_rows, visit_unit, before_columns, per_dev, qtokens, pages)

    low_q = []
    for i in range(per_dev):
        wide = jnp.zeros((qtokens, width), F32)
        for c in range(per_dev):
            start = (c * per_dev + i) * qtokens
            wide += grads[i][c] * own_unit[start : start + qtokens]
            wide += grads[i][per_dev + c] * after_unit[start : start + qtokens]
        unit = q_unit[i * qtokens : (i + 1) * qtokens]
        out = (wide - unit * jnp.sum(unit * wide, axis=-1, keepdims=True)) * q_inv[i * qtokens : (i + 1) * qtokens]
        out = jnp.where(split == 0, out[:tokens], out[tokens:])
        d_query_ref[i] = out
        low_q.append(out.astype(BF16))

    low_p = []
    for c in range(per_dev):
        values = jnp.concatenate(
            [grads[i][c] * q_low[i * qtokens : (i + 1) * qtokens] for i in range(per_dev)]
            + [before_grads[i][per_dev + c] * before_q[i * qtokens : (i + 1) * qtokens] for i in range(per_dev)],
            axis=0,
        )
        high = values.astype(BF16)
        rest = (values - high.astype(F32)).astype(BF16)
        spots = slot_row(idx_ref, c) - split * patches
        table = (lax.broadcasted_iota(jnp.int32, (patches, slots), 0) == spots).astype(BF16)
        both = jnp.dot(table, jnp.concatenate([high, rest], axis=1), preferred_element_type=F32)
        wide = both[:, :width] + both[:, width:]
        page = half_ref[c].astype(F32)
        inv = inverse_norm(page)
        unit = page * inv
        out = (wide - unit * jnp.sum(unit * wide, axis=-1, keepdims=True)) * inv
        d_page_ref[c] = out
        low_p.append(out.astype(BF16))

    dims = (((0,), (0,)), ((), ()))
    total = jnp.zeros((width, qhid_ref.shape[2]), F32)
    for i in range(per_dev):
        total += lax.dot_general(low_q[i], qhid_ref[i], dims, preferred_element_type=F32)
    for c in range(per_dev):
        copies[c].wait()
        total += lax.dot_general(low_p[c], hid[c], dims, preferred_element_type=F32)
    groups, rows = keep_ref.shape[0], keep_ref.shape[1]
    partial = total.T.reshape(groups, 2, rows, width)
    keep_ref[...] = jnp.where(even, partial[:, 0], partial[:, 1])
    send_ref[...] = jnp.where(even, partial[:, 1], partial[:, 0]).astype(BF16)


def shards(page_hidden, query_hidden, page_pre, query_pre, match_index, positive):
    per_dev, _, width = page_pre.shape
    qtokens = query_pre.shape[1]
    patches = page_hidden.shape[1]
    hidden = page_hidden.shape[2]
    groups = lax.axis_size("blk")
    blocks = groups * 2
    pages = blocks * per_dev
    slots = match_index.shape[1] * match_index.shape[2]
    split = lax.axis_index("mp")
    vmem = pl.BlockSpec(memory_space=pltpu.VMEM)
    smem = pl.BlockSpec(memory_space=pltpu.SMEM)
    count = per_dev * (slots // 2) + per_dev * qtokens + 16
    payload = jax.ShapeDtypeStruct((count, width), BF16)
    first, second, rows = pl.pallas_call(
        functools.partial(gather_kernel, blocks),
        out_shape=(payload, payload, jax.ShapeDtypeStruct((per_dev * slots, width), BF16)),
        in_specs=[smem, vmem, vmem, vmem],
        out_specs=(vmem, vmem, vmem),
        compiler_params=pltpu.CompilerParams(vmem_limit_bytes=32 * 2**20),
        name="gather_rows",
    )(positive, match_index, page_pre, query_pre)
    swap = [(i, i ^ 1) for i in range(blocks)]
    cross = [(i, (i + 1) % blocks if i % 2 else (i - 1) % blocks) for i in range(blocks)]
    second = lax.ppermute(second, ("blk", "core"), cross)
    first = lax.ppermute(first, ("blk", "core"), swap)
    half = lax.dynamic_slice_in_dim(page_pre, split * patches, patches, 1)
    share = hidden // (2 * groups)
    d_page, d_query, send, keep = pl.pallas_call(
        functools.partial(main_kernel, pages),
        out_shape=(
            jax.ShapeDtypeStruct((per_dev, patches, width), F32),
            jax.ShapeDtypeStruct((per_dev, query_hidden.shape[1], width), F32),
            jax.ShapeDtypeStruct((groups, share, width), BF16),
            jax.ShapeDtypeStruct((groups, share, width), F32),
        ),
        in_specs=[smem] + [vmem] * 7 + [pl.BlockSpec(memory_space=pl.ANY)],
        out_specs=(vmem, vmem, vmem, vmem),
        scratch_shapes=[pltpu.VMEM(page_hidden.shape, BF16), pltpu.SemaphoreType.DMA((per_dev,))],
        compiler_params=pltpu.CompilerParams(vmem_limit_bytes=48 * 2**20),
        name="grads_and_partial",
    )(positive, match_index, first, second, rows, query_pre, half, query_hidden, page_hidden)
    got = lax.ppermute(send, "core", [(0, 1), (1, 0)])
    pair = (keep + got.astype(F32)).astype(BF16).reshape(groups * 2, share // 2, width)
    parts = lax.all_to_all(pair, ("blk", "mp"), 0, 0, tiled=True)
    return d_page, d_query, jnp.sum(parts.astype(F32), axis=0)


def solution(mesh):
    blocks, parts = mesh.devices.shape
    fine = Mesh(mesh.devices.reshape(blocks // 2, 2, parts), ("blk", "core", "mp"))
    dp = ("blk", "core")
    placed = (
        P(dp, "mp", None),
        P(dp, "mp", None),
        P(dp, None, None),
        P(dp, None, None),
        P(dp, None, None),
        P(dp),
    )
    return jax.shard_map(
        shards,
        mesh=fine,
        in_specs=placed,
        out_specs=(P(dp, "mp", None), P(dp, "mp", None), P(("blk", "core", "mp"), None)),
        check_vma=False,
    )
```

time: 309 us -> 49.3 us (0.16)
  waiting for transfers between devices: 261 us -> 15.5 us
  between operations: 14.2 us -> 0.78 us
  starting transfers between devices: 6.53 us -> 18.8 us
  matrix products: 7.38 us -> 0 us
  other arithmetic: 7.71 us -> 1.49 us
  Pallas kernels: 0 us -> 3.92 us
    unnamed x2 -> x0, waiting for transfers between devices: 253 us -> none
    all_to_all x0 -> x1, waiting for transfers between devices: none -> 14 us  [shards(): parts = lax.all_to_all(pair, ('blk', 'mp'), 0, 0, tiled=True)]
    all_to_all x0 -> x1, starting transfers between devices: none -> 13.6 us  [shards(): parts = lax.all_to_all(pair, ('blk', 'mp'), 0, 0, tiled=True)]
    dot_general x5 -> x0, matrix products: 7.38 us -> none  [the longest x2 6.43 us: contract_rows(): lax.dot_general(left, right, (((0,), (0,)), ((), ())), preferred_element_...]
    ppermute x4 -> x3, waiting for transfers between devices: 8.27 us -> 1.53 us  [the longest x1 1.52 us: shards(): got = lax.ppermute(send, 'core', [(0, 1), (1, 0)])]
    unnamed x9 -> x17, local copies, waits for them, and re-layouts: 2.67 us -> 8.4 us
    pallas_call x0 -> x2, Pallas kernels: none -> 3.92 us  [the longest x1 2.92 us: shards(): pl.pallas_call(functools.partial(main_kernel, pages), out_shape=(jax.Shap...]
    convert_element_type x1 -> x0, local copies, waits for them, and re-layouts: 3.85 us -> none  [shards(): emb_p = unit_p.astype(jnp.bfloat16)]
  transfers between devices with their start and end apart: 5 -> 4, of which waited for: 3 -> 2; matrix products, arithmetic and copies ran while one was open for 6% -> 11% of each run, Pallas kernels for 0% -> 0%
where the time goes in v1:
time: 49.3 us; the launch traced here: 49 us
  starting transfers between devices  18.8 us (38%)
  waiting for transfers between devices  15.5 us (31%)
  local copies, waits for them, and re-layouts  8.48 us (17%)
  Pallas kernels  3.92 us (8%)
  other arithmetic  1.49 us (3%)
  between operations  0.78 us (2%)
    all_to_all x1, waiting for transfers between devices, shards(): parts = lax.all_to_all(pair, ('blk', 'mp'), 0, 0, tiled=True)  14 us
    all_to_all x1, starting transfers between devices, shards(): parts = lax.all_to_all(pair, ('blk', 'mp'), 0, 0, tiled=True)  13.6 us
    unnamed x17, local copies, waits for them, and re-layouts  8.4 us
    ppermute x1, starting transfers between devices, shards(): second = lax.ppermute(second, ('blk', 'core'), cross)  5.04 us
    pallas_call x1, Pallas kernels, shards(): pl.pallas_call(functools.partial(main_kernel, pages), out_shape=(jax.Shap...  2.92 us
    ppermute x1, waiting for transfers between devices, shards(): got = lax.ppermute(send, 'core', [(0, 1), (1, 0)])  1.52 us
    pallas_call x1, Pallas kernels, shards(): pl.pallas_call(functools.partial(gather_kernel, blocks), out_shape=(paylo...  0.99 us
  transfers between devices with their start and end apart: 4, of which 2 were waited for; matrix products, arithmetic and copies ran while one was open for 11% of the time, Pallas kernels for 0%

profile of v1, /device:TPU:32, one launch (start us, length us, event | category | flops | bytes accessed | tf_op | source)
XLA Modules:
  0.0 49.0 jit_solution(10043302298672373595)
XLA Ops:
  0.6 1.1 %copy.9.page_ref = bf16[2,1030,128]{2,1,0:T(8,128)(2,1)S(1)} copy(bf16[2,1030,128]{2,0,1:T(2,128)(2,1)} %param.8) | data formatting | bytes 1054720 | tf_op args[2]
  1.7 0.0 copy-start.1
  1.8 0.7 %copy-done.1 = bf16[2,32,128]{2,1,0:T(8,128)(2,1)S(1)} copy-done((bf16[2,32,128]{2,1,0:T(8,128)(2,1)S(1)}, bf16[2,32,128]{2,1,0:T(8,128)(2,1)}, u32[]{:S(2)}) %copy-start.1) | copy-done | bytes 16408
  2.5 0.0 copy-start.3
  2.5 0.7 %copy-done.3 = s32[2,2,64]{2,1,0:T(2,128)S(1)} copy-done((s32[2,2,64]{2,1,0:T(2,128)S(1)}, s32[2,2,64]{2,1,0:T(2,128)}, u32[]{:S(2)}) %copy-start.3) | copy-done | bytes 1048
  3.1 0.0 copy-start.5
  3.2 0.7 %copy-done.5 = s32[2]{0:T(128)S(1)} copy-done((s32[2]{0:T(128)S(1)}, s32[2]{0:T(128)}, u32[]{:S(2)}) %copy-start.5) | copy-done | bytes 32
  3.8 1.0 %gather_rows.1 = (bf16[208,128]{1,0:T(8,128)(2,1)S(1)}, bf16[208,128]{1,0:T(8,128)(2,1)S(1)}, bf16[256,128]{1,0:T(8,128)(2,1)S(1)}) custom-call(s32[2]{0:T(128)S(1)} %copy-done.5, s32[2,2,64]{2,1,0:T(2,128)S(1)} %copy-done.3, bf16[2,1030,128]{2,1,0:T(8,128)(2,1)S(1)} %copy.9.page_ref, bf16[2,32,128]{2,1,0:T(8,128)(2,1)S(1)} %copy-done.1), custom_call_target="tpu_custom_call" | custom-call | tf_op jit(solution)/shard_map/gather_rows/pallas_call | solution.py:190
  4.8 0.1 collective-permute-start
  4.9 5.0 %collective-permute-start.1 = (bf16[208,128]{1,0:T(8,128)(2,1)S(1)}, bf16[208,128]{1,0:T(8,128)(2,1)S(1)}, u32[]{:S(2)}, u32[]{:S(2)}) collective-permute-start(bf16[208,128]{1,0:T(8,128)(2,1)S(1)} %get-tuple-element.11), channel_id=1, source_target_pairs={{0,254},{2,4},{4,2},{6,8},{8,6},{10,12},{12,10},{14,16},{16,14},{1... | collective-permute-start | bytes 159752 | tf_op jit(solution)/shard_map/ppermute | solution.py:200
  9.9 0.1 constant_dynamic-slice_fusion.half_ref
  10.0 0.0 copy-start
  10.0 0.0 copy-start.2
  10.0 0.0 copy-start.4
  10.1 0.0 copy-start.6
  10.1 4.1 %copy.11.hid_ref = bf16[2,515,2048]{2,1,0:T(8,128)(2,1)S(1)} copy(bf16[2,515,2048]{2,0,1:T(2,128)(2,1)} %param.6) | data formatting | bytes 8437760 | tf_op args[0]
  14.2 0.0 collective-permute-done.first_ref
  14.2 0.0 collective-permute-done.1.second_ref
  14.2 0.0 copy-done
  14.3 0.0 copy-done.2
  14.3 0.0 copy-done.4
  14.3 0.0 copy-done.6
  14.3 2.9 %grads_and_partial.1 = (f32[2,515,128]{2,1,0:T(8,128)S(1)}, f32[2,16,128]{2,1,0:T(8,128)}, bf16[64,16,128]{2,1,0:T(8,128)(2,1)S(1)}, f32[64,16,128]{2,1,0:T(8,128)S(1)}) custom-call(s32[2]{0:T(128)S(1)} %copy-done.6, s32[2,2,64]{2,1,0:T(2,128)S(1)} %copy-done.4, bf16[208,128]{1,0:T(8,128)(2,1)S(1)} %collective-permute-done.first_ref, ...), custom_call_target="tpu_custom_call" | custom-call | tf_op jit(solution)/shard_map/grads_and_partial/pallas_call | solution.py:204
  17.2 0.1 collective-permute-start.2
  17.3 1.5 %collective-permute-done.2 = bf16[64,16,128]{2,1,0:T(8,128)(2,1)S(1)} collective-permute-done((bf16[64,16,128]{2,1,0:T(8,128)(2,1)S(1)}, bf16[64,16,128]{2,1,0:T(8,128)(2,1)S(1)}, u32[]{:S(2)}, u32[]{:S(2)}) %collective-permute-start.2) | collective-permute-done | bytes 262176 | tf_op jit(solution)/shard_map/ppermute | solution.py:218
  18.8 0.8 %add_convert_fusion = bf16[64,16,128]{2,1,0:T(8,128)(2,1)} fusion(f32[64,16,128]{2,1,0:T(8,128)S(1)} %get-tuple-element.15, bf16[64,16,128]{2,1,0:T(8,128)(2,1)S(1)} %collective-permute-done.2), kind=kLoop, calls=%fused_computation.1 | loop fusion | flops 393216 | bytes 1048576 | tf_op jit(solution)/shard_map/convert_element_type | solution.py:219
  19.6 13.6 %all-to-all-start = ((bf16[128,8,128]{2,1,0:T(8,128)(2,1)}), bf16[128,8,128]{2,1,0:T(8,128)(2,1)S(1)}, u32[]{:S(2)}, u32[]{:S(2)}) async-start(bf16[128,8,128]{2,1,0:T(8,128)(2,1)} %bitcast), calls=%async_computation | async-start | bytes 524288 | tf_op jit(solution)/shard_map/all_to_all | solution.py:220
  33.2 1.1 %copy.12 = f32[2,515,128]{2,0,1:T(2,128)} copy(f32[2,515,128]{2,1,0:T(8,128)S(1)} %get-tuple-element.17) | data formatting | bytes 1054720
  34.3 14.0 %all-to-all-done = bf16[128,8,128]{2,1,0:T(8,128)(2,1)S(1)} async-done(((bf16[128,8,128]{2,1,0:T(8,128)(2,1)}), bf16[128,8,128]{2,1,0:T(8,128)(2,1)S(1)}, u32[]{:S(2)}, u32[]{:S(2)}) %all-to-all-start) | async-done | bytes 262176 | tf_op jit(solution)/shard_map/all_to_all | solution.py:220
  48.2 0.7 %convert_reduce_fusion = f32[8,128]{1,0:T(8,128)} fusion(bf16[128,8,128]{2,1,0:T(8,128)(2,1)S(1)} %all-to-all-done), kind=kLoop, calls=%fused_computation | loop fusion | flops 261120 | bytes 266240 | tf_op jit(solution)/shard_map/reduce_sum | solution.py:221
Async XLA Ops:
  1.7 0.7 %copy-start.1 = (bf16[2,32,128]{2,1,0:T(8,128)(2,1)S(1)}, bf16[2,32,128]{2,1,0:T(8,128)(2,1)}, u32[]{:S(2)}) copy-start(bf16[2,32,128]{2,1,0:T(8,128)(2,1)} %query_ref.3) | copy-start | bytes 49156
  2.5 0.7 %copy-start.3 = (s32[2,2,64]{2,1,0:T(2,128)S(1)}, s32[2,2,64]{2,1,0:T(2,128)}, u32[]{:S(2)}) copy-start(s32[2,2,64]{2,1,0:T(2,128)} %idx_ref.3) | copy-start | bytes 3076
  3.1 0.7 %copy-start.5 = (s32[2]{0:T(128)S(1)}, s32[2]{0:T(128)}, u32[]{:S(2)}) copy-start(s32[2]{0:T(128)} %pos_ref.3) | copy-start | bytes 28
  4.8 9.4 %collective-permute-start = (bf16[208,128]{1,0:T(8,128)(2,1)S(1)}, bf16[208,128]{1,0:T(8,128)(2,1)S(1)}, u32[]{:S(2)}, u32[]{:S(2)}) collective-permute-start(bf16[208,128]{1,0:T(8,128)(2,1)S(1)} %get-tuple-element.10), channel_id=1, source_target_pairs={{0,2},{2,0},{4,6},{6,4},{8,10},{10,8},{12,14},{14,12},{16,18},{18,... | collective-permute-start | bytes 159752 | tf_op jit(solution)/shard_map/ppermute | solution.py:201
  4.9 9.3 %collective-permute-start.1 = (bf16[208,128]{1,0:T(8,128)(2,1)S(1)}, bf16[208,128]{1,0:T(8,128)(2,1)S(1)}, u32[]{:S(2)}, u32[]{:S(2)}) collective-permute-start(bf16[208,128]{1,0:T(8,128)(2,1)S(1)} %get-tuple-element.11), channel_id=1, source_target_pairs={{0,254},{2,4},{4,2},{6,8},{8,6},{10,12},{12,10},{14,16},{16,14},{1... | collective-permute-start | bytes 159752 | tf_op jit(solution)/shard_map/ppermute | solution.py:200
  10.0 4.2 %copy-start = (bf16[2,16,2048]{2,1,0:T(8,128)(2,1)S(1)}, bf16[2,16,2048]{2,1,0:T(8,128)(2,1)}, u32[]{:S(2)}) copy-start(bf16[2,16,2048]{2,1,0:T(8,128)(2,1)} %qhid_ref.1) | copy-start | bytes 393220
  10.0 4.2 %copy-start.2 = (bf16[2,32,128]{2,1,0:T(8,128)(2,1)S(1)}, bf16[2,32,128]{2,1,0:T(8,128)(2,1)}, u32[]{:S(2)}) copy-start(bf16[2,32,128]{2,1,0:T(8,128)(2,1)} %query_ref.3) | copy-start | bytes 49156
  10.0 4.2 %copy-start.4 = (s32[2,2,64]{2,1,0:T(2,128)S(1)}, s32[2,2,64]{2,1,0:T(2,128)}, u32[]{:S(2)}) copy-start(s32[2,2,64]{2,1,0:T(2,128)} %idx_ref.3) | copy-start | bytes 3076
  10.1 4.2 %copy-start.6 = (s32[2]{0:T(128)S(1)}, s32[2]{0:T(128)}, u32[]{:S(2)}) copy-start(s32[2]{0:T(128)} %pos_ref.3) | copy-start | bytes 28
  17.2 1.6 %collective-permute-start.2 = (bf16[64,16,128]{2,1,0:T(8,128)(2,1)S(1)}, bf16[64,16,128]{2,1,0:T(8,128)(2,1)S(1)}, u32[]{:S(2)}, u32[]{:S(2)}) collective-permute-start(bf16[64,16,128]{2,1,0:T(8,128)(2,1)S(1)} %get-tuple-element.16), channel_id=1, source_target_pairs={{0,2},{2,0},{1,3},{3,1},{4,6},{6,4},{5,7},{7,5},{8,10},{10,8},{9,1... | collective-permute-start | bytes 786440 | tf_op jit(solution)/shard_map/ppermute | solution.py:218
  19.6 28.6 %all-to-all-start = ((bf16[128,8,128]{2,1,0:T(8,128)(2,1)}), bf16[128,8,128]{2,1,0:T(8,128)(2,1)S(1)}, u32[]{:S(2)}, u32[]{:S(2)}) async-start(bf16[128,8,128]{2,1,0:T(8,128)(2,1)} %bitcast), calls=%async_computation | async-start | bytes 524288 | tf_op jit(solution)/shard_map/all_to_all | solution.py:220

commit v2 on v1

v2 whole, which is shorter than its diff:
```python
import functools

import jax
import jax.numpy as jnp
from jax import lax
from jax.experimental import pallas as pl
from jax.experimental.pallas import tpu as pltpu
from jax.sharding import Mesh, PartitionSpec as P

SCALE_LOGIT = 10.0
EPS = 1e-06
F32 = jnp.float32
BF16 = jnp.bfloat16
LANES = 128
RUN = 4
VMEM = pl.BlockSpec(memory_space=pltpu.VMEM)
ANY = pl.BlockSpec(memory_space=pl.ANY)


def one_hot(targets, rows):
    return (lax.broadcasted_iota(jnp.int32, (rows, targets.shape[1]), 0) == targets).astype(BF16)


def inverse_norm(wide):
    return lax.rsqrt(jnp.sum(wide * wide, axis=-1, keepdims=True) + EPS)


def rounded(wide):
    return wide.astype(BF16).astype(F32)


def rounded_unit(raw):
    wide = raw.astype(F32)
    return rounded(wide * inverse_norm(wide))


def place_kernel(out_ref):
    block = lax.axis_index("blk") * 2 + lax.axis_index("core")
    out_ref[...] = jnp.full(out_ref.shape, block, jnp.int32)


def gather_kernel(blocks, place_ref, idx_ref, pos_ref, query_ref, page_ref, first_ref, second_ref, rows_ref, half_ref, misc_ref):
    patches, per_dev, width = page_ref.shape
    flat = patches * per_dev
    half = idx_ref.shape[2]
    spots = jnp.concatenate(
        [idx_ref[c, v : v + 1, :] * per_dev + c for c in range(per_dev) for v in range(idx_ref.shape[1])], axis=1
    )
    target = pos_ref[...]
    rows = lax.dot_general(
        one_hot(spots, flat),
        page_ref[...].reshape(flat, width),
        (((0,), (0,)), ((), ())),
        preferred_element_type=F32,
    ).astype(BF16)
    rows_ref[...] = rows
    own = jnp.concatenate([rows[2 * c * half : (2 * c + 1) * half] for c in range(per_dev)], axis=0)
    visiting = jnp.concatenate([rows[(2 * c + 1) * half : (2 * c + 2) * half] for c in range(per_dev)], axis=0)
    even = lax.axis_index("core") == 0
    shift = target // per_dev - place_ref[0:1, :per_dev] + blocks
    column = jnp.where(shift >= blocks, shift - blocks, shift) * per_dev + target % per_dev
    count = own.shape[0]
    first_ref[0:count, :] = jnp.where(even, own, visiting)
    second_ref[0:count, :] = jnp.where(even, visiting, own)
    lane = lax.broadcasted_iota(jnp.int32, (16, width), 1)
    meta = jnp.zeros((16, width), F32)
    for i in range(per_dev):
        meta = jnp.where(lane == i, column[:, i : i + 1].astype(F32), meta)
    tail = jnp.concatenate([query_ref[...].reshape(-1, width), meta.astype(BF16)], axis=0)
    first_ref[count:, :] = tail
    second_ref[count:, :] = tail
    half_rows = half_ref.shape[0]
    start = lax.axis_index("mp") * half_rows
    half_ref[...] = page_ref[pl.ds(start, half_rows)]
    misc_ref[...] = jnp.broadcast_to(spots - start * per_dev, misc_ref.shape)


def local_kernel(
    sent_ref, rows_ref, half_ref, misc_ref, hid_ref, unit_ref, inv_ref, table_ref, own_ref, visit_ref, query_ref,
    qinv_ref, slot_unit_ref, slot_inv_ref, same_ref, picked_ref,
):
    patches, per_dev, width = half_ref.shape
    flat = patches * per_dev
    slots = rows_ref.shape[0]
    half = slots // (2 * per_dev)
    spots = misc_ref[0:1, :]
    table = one_hot(spots, flat)
    table_ref[...] = table
    page = half_ref[...].reshape(flat, width).astype(F32)
    inv = inverse_norm(page)
    unit_ref[...] = page * inv
    inv_ref[...] = jnp.broadcast_to(inv, (flat, width))
    wide = rows_ref[...].astype(F32)
    inv = inverse_norm(wide)
    slot_unit = wide * inv
    slot_unit_ref[...] = slot_unit
    for c in range(per_dev):
        own_ref[c * half : (c + 1) * half] = rounded(slot_unit[2 * c * half : (2 * c + 1) * half])
        visit_ref[c * half : (c + 1) * half] = rounded(slot_unit[(2 * c + 1) * half : (2 * c + 2) * half])
    column = misc_ref[...].astype(F32).T[:, 0:1]
    same = column == spots.astype(F32)
    earlier = lax.broadcasted_iota(jnp.int32, same.shape, 1) < lax.broadcasted_iota(jnp.int32, same.shape, 0)
    repeats = jnp.sum((same & earlier).astype(F32), axis=1, keepdims=True)
    counts = (repeats == 0) & (column >= 0) & (column < flat)
    same_ref[...] = same.astype(BF16)
    slot_inv_ref[...] = jnp.where(counts, inv, 0.0) + jnp.zeros((slots, width), F32)
    wide = sent_ref[per_dev * half : (per_dev + 1) * half, :].astype(F32)
    inv = inverse_norm(wide)
    query_ref[...] = wide * inv
    qinv_ref[...] = jnp.broadcast_to(inv, wide.shape)
    picked_ref[...] = lax.dot_general(
        table, hid_ref[...].reshape(flat, -1), (((0,), (0,)), ((), ())), preferred_element_type=F32
    ).astype(BF16)


def loss_grads(unit_q, own_rows, other_rows, columns, per_dev, qtokens, pages):
    grads = []
    for i in range(per_dev):
        query = unit_q[i * qtokens : (i + 1) * qtokens]
        scores = []
        for rows in (own_rows, other_rows):
            for c in range(per_dev):
                start = (c * per_dev + i) * qtokens
                prods = jnp.sum(query * rows[start : start + qtokens], axis=0, keepdims=True)
                scores.append(SCALE_LOGIT * jnp.sum(prods, axis=1, keepdims=True))
        top = functools.reduce(jnp.maximum, scores)
        parts = [jnp.exp(s - top) for s in scores]
        total = functools.reduce(jnp.add, parts)
        grads.append(
            [
                (part / total - (columns[i] == j).astype(F32)) * (SCALE_LOGIT / pages)
                for j, part in enumerate(parts)
            ]
        )
    return grads


def main_kernel(
    pages, per_dev, sent_ref, first_ref, second_ref, own_ref, visit_ref, query_ref, qinv_ref, slot_unit_ref,
    slot_inv_ref, same_ref, picked_ref, qhid_ref, d_query_ref, values_ref, send_ref, keep_ref,
):
    qcount, width = query_ref.shape
    qtokens = qcount // per_dev
    tokens = qhid_ref.shape[1]
    split = lax.axis_index("mp")
    even = lax.axis_index("core") == 0
    count = own_ref.shape[0]

    first, second = first_ref[...], second_ref[...]
    after = jnp.where(even, first[:count], second[:count])
    before = jnp.where(even, second, first)
    own_unit = own_ref[...]
    visit_unit = visit_ref[...]
    after_unit = rounded_unit(after)
    before_rows = rounded_unit(before[:count])
    before_q = rounded_unit(before[count : count + qcount])
    q_unit = query_ref[...]
    q_inv = qinv_ref[...]
    q_low = q_unit.astype(BF16).astype(F32)

    own_meta = sent_ref[count + qcount :, :].astype(F32)
    before_meta = before[count + qcount :].astype(F32)
    columns = [own_meta[0:1, i : i + 1] for i in range(per_dev)]
    before_columns = [before_meta[0:1, i : i + 1] for i in range(per_dev)]
    grads = loss_grads(q_low, own_unit, after_unit, columns, per_dev, qtokens, pages)
    before_grads = loss_grads(before_q, before_rows, visit_unit, before_columns, per_dev, qtokens, pages)

    values = []
    for c in range(per_dev):
        for i in range(per_dev):
            values.append(grads[i][c] * q_low[i * qtokens : (i + 1) * qtokens])
        for i in range(per_dev):
            values.append(before_grads[i][per_dev + c] * before_q[i * qtokens : (i + 1) * qtokens])
    values = jnp.concatenate(values, axis=0)
    high = values.astype(BF16)
    rest = (values - high.astype(F32)).astype(BF16)
    parts = jnp.concatenate([high, rest], axis=1)
    values_ref[...] = parts
    both = jnp.dot(same_ref[...], parts, preferred_element_type=F32)
    wide = both[:, :width] + both[:, width:]
    unit = slot_unit_ref[...]
    out = (wide - unit * jnp.sum(unit * wide, axis=-1, keepdims=True)) * slot_inv_ref[...]

    low = []
    for i in range(per_dev):
        wide_q = jnp.zeros((qtokens, width), F32)
        for c in range(per_dev):
            start = (c * per_dev + i) * qtokens
            wide_q += grads[i][c] * own_unit[start : start + qtokens]
            wide_q += grads[i][per_dev + c] * after_unit[start : start + qtokens]
        unit_i = q_unit[i * qtokens : (i + 1) * qtokens]
        out_q = (wide_q - unit_i * jnp.sum(unit_i * wide_q, axis=-1, keepdims=True)) * q_inv[
            i * qtokens : (i + 1) * qtokens
        ]
        out_q = jnp.where(split == 0, out_q[:tokens], out_q[tokens:])
        d_query_ref[i] = out_q
        low.append(out_q)
    low = jnp.concatenate(low, axis=0)
    total = jnp.dot(out.T.astype(BF16), picked_ref[...], preferred_element_type=F32)
    total += jnp.dot(
        low.T.astype(BF16), qhid_ref[...].reshape(per_dev * tokens, -1), preferred_element_type=F32
    )
    rows = keep_ref.shape[1]
    step = LANES // (2 * rows)
    for t in range(total.shape[1] // LANES):
        part = total[:, t * LANES : (t + 1) * LANES].T.reshape(step, 2, rows, width)
        keep_ref[t * step : (t + 1) * step] = jnp.where(even, part[:, 0], part[:, 1])
        send_ref[t * step : (t + 1) * step] = jnp.where(even, part[:, 1], part[:, 0]).astype(BF16)


def page_kernel(values_ref, table_ref, unit_ref, inv_ref, _keep_in, out_ref, _keep_out):
    width = unit_ref.shape[1]
    both = jnp.dot(table_ref[...], values_ref[...], preferred_element_type=F32)
    wide = both[:, :width] + both[:, width:]
    unit = unit_ref[...]
    out = (wide - unit * jnp.sum(unit * wide, axis=-1, keepdims=True)) * inv_ref[...]
    out_ref[...] = out.reshape(out_ref.shape)


def add_kernel(keep_ref, got_ref, out_ref):
    out_ref[...] = (keep_ref[...] + got_ref[...].astype(F32)).astype(BF16)


def sum_kernel(parts_ref, out_ref):
    total = jnp.sum(parts_ref[...].astype(F32), axis=0)
    rows = out_ref.shape[0]
    out_ref[...] = total[:rows] + total[rows:]


def shards(page_hidden, query_hidden, page_pre, query_pre, match_index, positive):
    per_dev, patches_all, width = page_pre.shape
    qtokens = query_pre.shape[1]
    patches = page_hidden.shape[1]
    hidden = page_hidden.shape[2]
    groups = lax.axis_size("blk")
    blocks = groups * 2
    pages = blocks * per_dev
    slots = per_dev * match_index.shape[1] * match_index.shape[2]
    page_t = jnp.transpose(page_pre, (1, 0, 2))
    hid_t = jnp.transpose(page_hidden, (1, 0, 2))
    limit = pltpu.CompilerParams(vmem_limit_bytes=24 * 2**20)
    place = pl.pallas_call(
        place_kernel,
        out_shape=jax.ShapeDtypeStruct((8, LANES), jnp.int32),
        out_specs=VMEM,
        compiler_params=limit,
        cost_estimate=pl.CostEstimate(flops=5 * 10**9, bytes_accessed=4096, transcendentals=0),
        name="place",
    )()
    count = slots // 2 + per_dev * qtokens + 16
    payload = jax.ShapeDtypeStruct((count, width), BF16)
    first, second, rows, half, misc = pl.pallas_call(
        functools.partial(gather_kernel, blocks),
        out_shape=(
            payload,
            payload,
            jax.ShapeDtypeStruct((slots, width), BF16),
            jax.ShapeDtypeStruct((patches, per_dev, width), BF16),
            jax.ShapeDtypeStruct((8, slots), jnp.int32),
        ),
        in_specs=[VMEM] * 5,
        out_specs=(VMEM,) * 5,
        compiler_params=limit,
        name="gather_rows",
    )(place, match_index, positive.reshape(1, per_dev), query_pre, page_t)
    swap = [(i, i ^ 1) for i in range(blocks)]
    cross = []
    for i in range(blocks):
        j = (i + 1) % blocks if i % 2 else (i - 1) % blocks
        for part in range(lax.axis_size("mp")):
            cross.append((2 * i + part, 2 * j + (part if i // (2 * RUN) == j // (2 * RUN) else 1 - part)))
    far = lax.ppermute(second, ("blk", "core", "mp"), cross)
    near = lax.ppermute(first, ("blk", "core"), swap)
    wide_rows = jax.ShapeDtypeStruct((patches * per_dev, width), F32)
    own_rows = jax.ShapeDtypeStruct((slots // 2, width), F32)
    own_queries = jax.ShapeDtypeStruct((per_dev * qtokens, width), F32)
    slot_rows = jax.ShapeDtypeStruct((slots, width), F32)
    unit, inv, table, *local = pl.pallas_call(
        local_kernel,
        out_shape=(
            wide_rows,
            wide_rows,
            jax.ShapeDtypeStruct((patches * per_dev, slots), BF16),
            own_rows,
            own_rows,
            own_queries,
            own_queries,
            slot_rows,
            slot_rows,
            jax.ShapeDtypeStruct((slots, slots), BF16),
            jax.ShapeDtypeStruct((slots, hidden), BF16),
        ),
        in_specs=[VMEM] * 5,
        out_specs=(VMEM,) * 11,
        compiler_params=limit,
        cost_estimate=pl.CostEstimate(flops=5 * 10**9, bytes_accessed=10**6, transcendentals=0),
        name="local_rows",
    )(first, rows, half, misc, hid_t)
    share = hidden // (2 * groups)
    d_query, values, send, keep = pl.pallas_call(
        functools.partial(main_kernel, pages, per_dev),
        out_shape=(
            jax.ShapeDtypeStruct((per_dev, query_hidden.shape[1], width), F32),
            jax.ShapeDtypeStruct((slots, 2 * width), BF16),
            jax.ShapeDtypeStruct((groups, share, width), BF16),
            jax.ShapeDtypeStruct((groups, share, width), F32),
        ),
        in_specs=[VMEM] * 12,
        out_specs=(VMEM,) * 4,
        compiler_params=limit,
        name="grads_and_partial",
    )(first, near, far, *local, query_hidden)
    got = lax.ppermute(send, "core", [(0, 1), (1, 0)])
    d_page, keep = pl.pallas_call(
        page_kernel,
        out_shape=(jax.ShapeDtypeStruct((patches, per_dev, width), F32), jax.ShapeDtypeStruct(keep.shape, F32)),
        in_specs=[VMEM] * 4 + [ANY],
        out_specs=(VMEM, ANY),
        input_output_aliases={4: 1},
        compiler_params=limit,
        cost_estimate=pl.CostEstimate(flops=10**9, bytes_accessed=10**6, transcendentals=0),
        name="page_grads",
    )(values, table, unit, inv, keep)
    small = pltpu.CompilerParams(vmem_limit_bytes=16 * 2**20)
    pair = pl.pallas_call(
        add_kernel,
        out_shape=jax.ShapeDtypeStruct(got.shape, BF16),
        in_specs=[VMEM, VMEM],
        out_specs=VMEM,
        compiler_params=small,
        name="add_pair",
    )(keep, got)
    parts = lax.all_to_all(pair.reshape(groups * 2, share // 2, width), ("blk", "mp"), 0, 0, tiled=True)
    grad = pl.pallas_call(
        sum_kernel,
        out_shape=jax.ShapeDtypeStruct((share // 2, width), F32),
        in_specs=[VMEM],
        out_specs=VMEM,
        compiler_params=small,
        name="sum_parts",
    )(parts.reshape(groups, share, width))
    return jnp.transpose(d_page, (1, 0, 2)), d_query, grad


def solution(mesh):
    blocks, parts = mesh.devices.shape
    fine = Mesh(mesh.devices.reshape(blocks // 2, 2, parts), ("blk", "core", "mp"))
    dp = ("blk", "core")
    placed = (
        P(dp, "mp", None),
        P(dp, "mp", None),
        P(dp, None, None),
        P(dp, None, None),
        P(dp, None, None),
        P(dp),
    )
    return jax.shard_map(
        shards,
        mesh=fine,
        in_specs=placed,
        out_specs=(P(dp, "mp", None), P(dp, "mp", None), P(("blk", "core", "mp"), None)),
        check_vma=False,
    )
```

time: 49.3 us -> 42.9 us (0.87)
  blocking collectives: 0 us -> 28.9 us
  starting transfers between devices: 18.8 us -> 4.3 us
  waiting for transfers between devices: 15.5 us -> 1.7 us
  local copies, waits for them, and re-layouts: 8.48 us -> 1.04 us
  Pallas kernels: 3.92 us -> 6.1 us
  other arithmetic: 1.49 us -> 0 us
    all_to_all x0 -> x1, blocking collectives: none -> 28.9 us  [shards(): lax.all_to_all(pair.reshape(groups * 2, share // 2, width), ('blk', 'mp')...]
    all_to_all x1 -> x0, waiting for transfers between devices: 14 us -> none  [shards(): parts = lax.all_to_all(pair, ('blk', 'mp'), 0, 0, tiled=True)]
    all_to_all x1 -> x0, starting transfers between devices: 13.6 us -> none  [shards(): parts = lax.all_to_all(pair, ('blk', 'mp'), 0, 0, tiled=True)]
    unnamed x17 -> x12, local copies, waits for them, and re-layouts: 8.4 us -> 1.04 us
    pallas_call x1 -> x6, Pallas kernels: 2.92 us -> 5.34 us  [the longest x1 2.15 us: shards(): pl.pallas_call(local_kernel, out_shape=(wide_rows, wide_rows, jax.ShapeDt...]
    ppermute x2, waiting for transfers between devices: 0.01 us -> 1.43 us  [the longest x1 1.42 us: shards(): far = lax.ppermute(second, ('blk', 'core', 'mp'), cross)]
    ppermute x1, waiting for transfers between devices: 1.52 us -> 0.28 us  [shards(): got = lax.ppermute(send, 'core', [(0, 1), (1, 0)])]
    ppermute x2, starting transfers between devices: 5.13 us -> 4.28 us  [the longest x1 4.28 us: shards(): far = lax.ppermute(second, ('blk', 'core', 'mp'), cross)]
  transfers between devices with their start and end apart: 4 -> 3, of which waited for: 2 -> 2; matrix products, arithmetic and copies ran while one was open for 11% -> 0% of each run, Pallas kernels for 0% -> 8%
where the time goes in v2:
time: 42.9 us; the launch traced here: 42.7 us
  blocking collectives  28.9 us (67%)
  Pallas kernels  6.1 us (14%)
  starting transfers between devices  4.3 us (10%)
  waiting for transfers between devices  1.7 us (4%)
  local copies, waits for them, and re-layouts  1.04 us (2%)
  between operations  0.71 us (2%)
    all_to_all x1, blocking collectives, shards(): lax.all_to_all(pair.reshape(groups * 2, share // 2, width), ('blk', 'mp')...  28.9 us
    ppermute x1, starting transfers between devices, shards(): far = lax.ppermute(second, ('blk', 'core', 'mp'), cross)  4.28 us
    pallas_call x1, Pallas kernels, shards(): pl.pallas_call(local_kernel, out_shape=(wide_rows, wide_rows, jax.ShapeDt...  2.15 us
    ppermute x1, waiting for transfers between devices, shards(): far = lax.ppermute(second, ('blk', 'core', 'mp'), cross)  1.42 us
    pallas_call x1, Pallas kernels, shards(): pl.pallas_call(page_kernel, out_shape=(jax.ShapeDtypeStruct((patches, per...  1.25 us
    pallas_call x1, Pallas kernels, shards(): pl.pallas_call(functools.partial(main_kernel, pages, per_dev), out_shape=...  1.23 us
    unnamed x12, local copies, waits for them, and re-layouts  1.04 us
  transfers between devices with their start and end apart: 3, of which 2 were waited for; matrix products, arithmetic and copies ran while one was open for 0% of the time, Pallas kernels for 8%

profile of v2, /device:TPU:32, one launch (start us, length us, event | category | flops | bytes accessed | tf_op | source)
XLA Modules:
  0.0 42.7 jit_solution(5795380458087703096)
XLA Ops:
  0.6 0.0 copy-start.4
  0.6 0.0 copy-start.3
  0.7 0.0 copy-start.2
  0.7 0.0 copy-start
  0.7 0.0 copy-start.5
  0.7 0.6 %copy-done.4 = s32[2]{0:T(128)S(1)} copy-done((s32[2]{0:T(128)S(1)}, s32[2]{0:T(128)}, u32[]{:S(2)}) %copy-start.4) | copy-done | bytes 32
  1.3 0.0 copy-done.3
  1.3 0.1 copy-done.2
  1.4 0.3 copy-done
  1.7 0.8 %gather_rows.1 = (bf16[208,128]{1,0:T(8,128)(2,1)S(1)}, bf16[208,128]{1,0:T(8,128)(2,1)S(1)}, bf16[256,128]{1,0:T(8,128)(2,1)S(1)}, bf16[515,2,128]{2,1,0:T(2,128)(2,1)S(1)}, s32[8,256]{1,0:T(8,128)S(1)}) custom-call(s32[8,128]{1,0:T(8,128)S(1)} %place.1.place_ref, s32[2,2,64]{2,1,0:T(2,128)S(1)} %copy-done.3, s32[1,2]{1,0:T(1,128)S(1)} %bitcast.9, ...), custom_call_target="tpu_custom_call" | custom-call | tf_op jit(solution)/shard_map/gather_rows/pallas_call | solution.py:252
  2.5 4.3 %collective-permute-start.1 = (bf16[208,128]{1,0:T(8,128)(2,1)S(1)}, bf16[208,128]{1,0:T(8,128)(2,1)S(1)}, u32[]{:S(2)}, u32[]{:S(2)}) collective-permute-start(bf16[208,128]{1,0:T(8,128)(2,1)S(1)} %get-tuple-element.26), channel_id=1, source_target_pairs={{0,255},{1,254},{2,4},{3,5},{4,2},{5,3},{6,8},{7,9},{8,6},{9,7},{1... | collective-permute-start | bytes 159752 | tf_op jit(solution)/shard_map/ppermute | solution.py:272
  6.8 0.0 collective-permute-start
  6.8 0.0 copy-done.5
  6.8 0.0 copy-start.1
  6.8 2.1 %local_rows.1 = (f32[1030,128]{1,0:T(8,128)S(1)}, f32[1030,128]{1,0:T(8,128)S(1)}, bf16[1030,256]{1,0:T(8,128)(2,1)S(1)}, f32[128,128]{1,0:T(8,128)S(1)}, f32[12...) custom-call(bf16[208,128]{1,0:T(8,128)(2,1)S(1)} %get-tuple-element., ...), custom_call_target="tpu_custom_call" | custom-call | flops 5000000000 | bytes 1000000 | tf_op jit(solution)/shard_map/local_rows/pallas_call | solution.py:278
  8.9 1.4 %collective-permute-done.1.second_ref = bf16[208,128]{1,0:T(8,128)(2,1)S(1)} collective-permute-done((bf16[208,128]{1,0:T(8,128)(2,1)S(1)}, bf16[208,128]{1,0:T(8,128)(2,1)S(1)}, u32[]{:S(2)}, u32[]{:S(2)}) %collective-permute-start.1) | collective-permute-done | bytes 53280 | tf_op jit(solution)/shard_map/ppermute | solution.py:272
  10.4 0.0 collective-permute-done.first_ref
  10.4 0.0 copy-done.1
  10.4 1.2 %grads_and_partial.1 = (f32[2,16,128]{2,1,0:T(8,128)}, bf16[256,256]{1,0:T(8,128)(2,1)S(1)}, bf16[64,16,128]{2,1,0:T(8,128)(2,1)S(1)}, f32[64,16,128]{2,1,0:T(8,128)S(1)}) custom-call(bf16[208,128]{1,0:T(8,128)(2,1)S(1)} %get-tuple-element.25.sent_ref, bf16[208,128]{1,0:T(8,128)(2,1)S(1)} %collective-permute-done.first_ref, ...), custom_call_target="tpu_custom_call" | custom-call | tf_op jit(solution)/shard_map/grads_and_partial/pallas_call | solution.py:300
  11.6 0.0 collective-permute-start.2
  11.6 1.2 %page_grads.1 = (f32[515,2,128]{2,1,0:T(2,128)}, f32[64,16,128]{2,1,0:T(8,128)S(1)}) custom-call(bf16[256,256]{1,0:T(8,128)(2,1)S(1)} %get-tuple-element.38.values_ref, bf16[1030,256]{1,0:T(8,128)(2,1)S(1)} %get-tuple-element.39.table_ref, f32[1030,128]{1,0:T(8,128)S(1)} %get-tuple-element.40.unit_ref, ...), custom_call_target="tpu_custom_call", output_to_operand_aliasing={{1}: (4, {})} | custom-call | flops 1000000000 | bytes 1000000 | tf_op jit(solution)/shard_map/page_grads/pallas_call | solution.py:314
  12.9 0.3 collective-permute-done.2.got_ref
  13.2 28.9 %all_to_all.5 = bf16[128,8,128]{2,1,0:T(8,128)(2,1)S(1)} all-to-all(bf16[128,8,128]{2,1,0:T(8,128)(2,1)S(1)} %bitcast.7), channel_id=1, replica_groups=mesh['blk'=64,'core'=2,'mp'=2] {'blk','mp'}, dimensions={0} | all-to-all | bytes 524288 | tf_op jit(solution)/shard_map/all_to_all | solution.py:333
  42.1 0.7 %sum_parts.1 = f32[8,128]{1,0:T(8,128)} custom-call(bf16[64,16,128]{2,1,0:T(8,128)(2,1)S(1)} %bitcast.6), custom_call_target="tpu_custom_call" | custom-call | tf_op jit(solution)/shard_map/sum_parts/pallas_call | solution.py:334
  (2 shorter events, 0.1 us)
Async XLA Ops:
  0.6 0.7 %copy-start.4 = (s32[2]{0:T(128)S(1)}, s32[2]{0:T(128)}, u32[]{:S(2)}) copy-start(s32[2]{0:T(128)} %param.11) | copy-start | bytes 28
  0.6 0.7 %copy-start.3 = (s32[2,2,64]{2,1,0:T(2,128)S(1)}, s32[2,2,64]{2,1,0:T(2,128)}, u32[]{:S(2)}) copy-start(s32[2,2,64]{2,1,0:T(2,128)} %idx_ref.1) | copy-start | bytes 3076
  0.7 0.7 %copy-start.2 = (bf16[2,32,128]{2,1,0:T(8,128)(2,1)S(1)}, bf16[2,32,128]{2,1,0:T(8,128)(2,1)}, u32[]{:S(2)}) copy-start(bf16[2,32,128]{2,1,0:T(8,128)(2,1)} %query_ref.1) | copy-start | bytes 49156
  0.7 1.1 %copy-start = (bf16[2,1030,128]{2,0,1:T(2,128)(2,1)S(1)}, bf16[2,1030,128]{2,0,1:T(2,128)(2,1)}, u32[]{:S(2)}) copy-start(bf16[2,1030,128]{2,0,1:T(2,128)(2,1)} %param.8) | copy-start | bytes 1582084
  0.7 6.1 %copy-start.5 = (bf16[2,515,2048]{2,0,1:T(2,128)(2,1)S(1)}, bf16[2,515,2048]{2,0,1:T(2,128)(2,1)}, u32[]{:S(2)}) copy-start(bf16[2,515,2048]{2,0,1:T(2,128)(2,1)} %param.6) | copy-start | bytes 12656644
  2.5 7.9 %collective-permute-start.1 = (bf16[208,128]{1,0:T(8,128)(2,1)S(1)}, bf16[208,128]{1,0:T(8,128)(2,1)S(1)}, u32[]{:S(2)}, u32[]{:S(2)}) collective-permute-start(bf16[208,128]{1,0:T(8,128)(2,1)S(1)} %get-tuple-element.26), channel_id=1, source_target_pairs={{0,255},{1,254},{2,4},{3,5},{4,2},{5,3},{6,8},{7,9},{8,6},{9,7},{1... | collective-permute-start | bytes 159752 | tf_op jit(solution)/shard_map/ppermute | solution.py:272
  6.8 3.6 %collective-permute-start = (bf16[208,128]{1,0:T(8,128)(2,1)S(1)}, bf16[208,128]{1,0:T(8,128)(2,1)S(1)}, u32[]{:S(2)}, u32[]{:S(2)}) collective-permute-start(bf16[208,128]{1,0:T(8,128)(2,1)S(1)} %get-tuple-element.25.sent_ref), channel_id=1, source_target_pairs={{0,2},{2,0},{4,6},{6,4},{8,10},{10,8},{12,14},{14,12},{16,18},{18,... | collective-permute-start | bytes 159752 | tf_op jit(solution)/shard_map/ppermute | solution.py:273
  6.8 3.6 %copy-start.1 = (bf16[2,16,2048]{2,1,0:T(8,128)(2,1)S(1)}, bf16[2,16,2048]{2,1,0:T(8,128)(2,1)}, u32[]{:S(2)}) copy-start(bf16[2,16,2048]{2,1,0:T(8,128)(2,1)} %qhid_ref.1) | copy-start | bytes 393220
  11.6 1.5 %collective-permute-start.2 = (bf16[64,16,128]{2,1,0:T(8,128)(2,1)S(1)}, bf16[64,16,128]{2,1,0:T(8,128)(2,1)S(1)}, u32[]{:S(2)}, u32[]{:S(2)}) collective-permute-start(bf16[64,16,128]{2,1,0:T(8,128)(2,1)S(1)} %get-tuple-element.46), channel_id=1, source_target_pairs={{0,2},{2,0},{1,3},{3,1},{4,6},{6,4},{5,7},{7,5},{8,10},{10,8},{9,1... | collective-permute-start | bytes 786440 | tf_op jit(solution)/shard_map/ppermute | solution.py:313

commit v3 on v2

--- a/solution.py
+++ b/solution.py
@@ -13,12 +13,16 @@
 BF16 = jnp.bfloat16
 LANES = 128
 RUN = 4
+PLANES = 8
+BLK = ("z2", "z1", "z0", "run")
+DP = BLK + ("core",)
 VMEM = pl.BlockSpec(memory_space=pltpu.VMEM)
 ANY = pl.BlockSpec(memory_space=pl.ANY)
 
 
 def one_hot(targets, rows):
-    return (lax.broadcasted_iota(jnp.int32, (rows, targets.shape[1]), 0) == targets).astype(BF16)
+    at = lax.broadcasted_iota(jnp.int16, (rows, targets.shape[1]), 0)
+    return jnp.where(at == targets.astype(jnp.int16), jnp.ones((), BF16), jnp.zeros((), BF16))
 
 
 def inverse_norm(wide):
@@ -35,7 +39,7 @@
 
 
 def place_kernel(out_ref):
-    block = lax.axis_index("blk") * 2 + lax.axis_index("core")
+    block = lax.axis_index(DP)
     out_ref[...] = jnp.full(out_ref.shape, block, jnp.int32)
 
 
@@ -76,8 +80,8 @@
 
 
 def local_kernel(
-    sent_ref, rows_ref, half_ref, misc_ref, hid_ref, unit_ref, inv_ref, table_ref, own_ref, visit_ref, query_ref,
-    qinv_ref, slot_unit_ref, slot_inv_ref, same_ref, picked_ref,
+    sent_ref, rows_ref, half_ref, misc_ref, hid_ref, qhid_ref, unit_ref, inv_ref, table_ref, own_ref, visit_ref, query_ref,
+    qinv_ref, slot_unit_ref, slot_inv_ref, same_ref, there_ref, here_ref,
 ):
     patches, per_dev, width = half_ref.shape
     flat = patches * per_dev
@@ -108,9 +112,17 @@
     inv = inverse_norm(wide)
     query_ref[...] = wide * inv
     qinv_ref[...] = jnp.broadcast_to(inv, wide.shape)
-    picked_ref[...] = lax.dot_general(
-        table, hid_ref[...].reshape(flat, -1), (((0,), (0,)), ((), ())), preferred_element_type=F32
-    ).astype(BF16)
+    dims = (((0,), (0,)), ((), ()))
+    tokens = qhid_ref.shape[0] * qhid_ref.shape[1]
+    eye = one_hot(lax.broadcasted_iota(jnp.int32, (1, tokens), 1), tokens)
+    picked = lax.dot_general(hid_ref[...].reshape(flat, -1), table, dims, preferred_element_type=F32)
+    turned = lax.dot_general(qhid_ref[...].reshape(tokens, -1), eye, dims, preferred_element_type=F32)
+    even = lax.axis_index("core") == 0
+    groups, share, _ = here_ref.shape
+    for part, at in ((picked, slice(0, slots)), (turned, slice(slots, slots + tokens))):
+        part = part.astype(BF16).reshape(groups, 2, share, part.shape[1])
+        here_ref[:, :, at] = jnp.where(even, part[:, 0], part[:, 1])
+        there_ref[:, :, at] = jnp.where(even, part[:, 1], part[:, 0])
 
 
 def loss_grads(unit_q, own_rows, other_rows, columns, per_dev, qtokens, pages):
@@ -135,13 +147,19 @@
     return grads
 
 
+def partial_sum(hid_ref, low):
+    groups, share, depth = hid_ref.shape
+    total = jnp.dot(hid_ref[...].reshape(groups * share, depth), low, preferred_element_type=F32)
+    return total.reshape(groups, share, low.shape[1])
+
+
 def main_kernel(
     pages, per_dev, sent_ref, first_ref, second_ref, own_ref, visit_ref, query_ref, qinv_ref, slot_unit_ref,
-    slot_inv_ref, same_ref, picked_ref, qhid_ref, d_query_ref, values_ref, send_ref, keep_ref,
+    slot_inv_ref, same_ref, there_ref, d_query_ref, values_ref, low_ref, send_ref,
 ):
     qcount, width = query_ref.shape
     qtokens = qcount // per_dev
-    tokens = qhid_ref.shape[1]
+    tokens = d_query_ref.shape[1]
     split = lax.axis_index("mp")
     even = lax.axis_index("core") == 0
     count = own_ref.shape[0]
@@ -195,30 +213,33 @@
         out_q = jnp.where(split == 0, out_q[:tokens], out_q[tokens:])
         d_query_ref[i] = out_q
         low.append(out_q)
-    low = jnp.concatenate(low, axis=0)
-    total = jnp.dot(out.T.astype(BF16), picked_ref[...], preferred_element_type=F32)
-    total += jnp.dot(
-        low.T.astype(BF16), qhid_ref[...].reshape(per_dev * tokens, -1), preferred_element_type=F32
-    )
-    rows = keep_ref.shape[1]
-    step = LANES // (2 * rows)
-    for t in range(total.shape[1] // LANES):
-        part = total[:, t * LANES : (t + 1) * LANES].T.reshape(step, 2, rows, width)
-        keep_ref[t * step : (t + 1) * step] = jnp.where(even, part[:, 0], part[:, 1])
-        send_ref[t * step : (t + 1) * step] = jnp.where(even, part[:, 1], part[:, 0]).astype(BF16)
-
-
-def page_kernel(values_ref, table_ref, unit_ref, inv_ref, _keep_in, out_ref, _keep_out):
+    low = jnp.concatenate([out] + low, axis=0).astype(BF16)
+    low_ref[...] = low
+    send_ref[...] = partial_sum(there_ref, low).astype(BF16)
+
+
+def page_kernel(values_ref, low_ref, here_ref, table_ref, unit_ref, inv_ref, query_ref, out_hbm, d_query_hbm, keep_ref, out_ref, sem):
     width = unit_ref.shape[1]
+    small = pltpu.make_async_copy(query_ref, d_query_hbm, sem.at[0])
+    small.start()
     both = jnp.dot(table_ref[...], values_ref[...], preferred_element_type=F32)
     wide = both[:, :width] + both[:, width:]
     unit = unit_ref[...]
     out = (wide - unit * jnp.sum(unit * wide, axis=-1, keepdims=True)) * inv_ref[...]
     out_ref[...] = out.reshape(out_ref.shape)
+    copy = pltpu.make_async_copy(out_ref, out_hbm, sem.at[1])
+    copy.start()
+    keep_ref[...] = partial_sum(here_ref, low_ref[...])
+    small.wait()
+    copy.wait()
 
 
 def add_kernel(keep_ref, got_ref, out_ref):
-    out_ref[...] = (keep_ref[...] + got_ref[...].astype(F32)).astype(BF16)
+    size = keep_ref.shape[0] // PLANES
+    for z in range(PLANES):
+        at = ((z & 1) * 4 + (z & 2) + (z >> 2)) * size
+        here = slice(z * size, (z + 1) * size)
+        out_ref[at : at + size] = (keep_ref[here] + got_ref[here].astype(F32)).astype(BF16)
 
 
 def sum_kernel(parts_ref, out_ref):
@@ -232,7 +253,7 @@
     qtokens = query_pre.shape[1]
     patches = page_hidden.shape[1]
     hidden = page_hidden.shape[2]
-    groups = lax.axis_size("blk")
+    groups = lax.axis_size(BLK)
     blocks = groups * 2
     pages = blocks * per_dev
     slots = per_dev * match_index.shape[1] * match_index.shape[2]
@@ -269,13 +290,16 @@
         j = (i + 1) % blocks if i % 2 else (i - 1) % blocks
         for part in range(lax.axis_size("mp")):
             cross.append((2 * i + part, 2 * j + (part if i // (2 * RUN) == j // (2 * RUN) else 1 - part)))
-    far = lax.ppermute(second, ("blk", "core", "mp"), cross)
-    near = lax.ppermute(first, ("blk", "core"), swap)
+    far = lax.ppermute(second, DP + ("mp",), cross)
+    near = lax.ppermute(first, DP, swap)
     wide_rows = jax.ShapeDtypeStruct((patches * per_dev, width), F32)
     own_rows = jax.ShapeDtypeStruct((slots // 2, width), F32)
     own_queries = jax.ShapeDtypeStruct((per_dev * qtokens, width), F32)
     slot_rows = jax.ShapeDtypeStruct((slots, width), F32)
-    unit, inv, table, *local = pl.pallas_call(
+    share = hidden // (2 * groups)
+    depth = slots + query_hidden.shape[0] * query_hidden.shape[1]
+    by_core = jax.ShapeDtypeStruct((groups, share, depth), BF16)
+    unit, inv, table, *local, here = pl.pallas_call(
         local_kernel,
         out_shape=(
             wide_rows,
@@ -288,39 +312,43 @@
             slot_rows,
             slot_rows,
             jax.ShapeDtypeStruct((slots, slots), BF16),
-            jax.ShapeDtypeStruct((slots, hidden), BF16),
+            by_core,
+            by_core,
         ),
-        in_specs=[VMEM] * 5,
-        out_specs=(VMEM,) * 11,
+        in_specs=[VMEM] * 6,
+        out_specs=(VMEM,) * 12,
         compiler_params=limit,
         cost_estimate=pl.CostEstimate(flops=5 * 10**9, bytes_accessed=10**6, transcendentals=0),
         name="local_rows",
-    )(first, rows, half, misc, hid_t)
-    share = hidden // (2 * groups)
-    d_query, values, send, keep = pl.pallas_call(
+    )(first, rows, half, misc, hid_t, query_hidden)
+    d_query, values, low, send = pl.pallas_call(
         functools.partial(main_kernel, pages, per_dev),
         out_shape=(
             jax.ShapeDtypeStruct((per_dev, query_hidden.shape[1], width), F32),
             jax.ShapeDtypeStruct((slots, 2 * width), BF16),
+            jax.ShapeDtypeStruct((depth, width), BF16),
             jax.ShapeDtypeStruct((groups, share, width), BF16),
+        ),
+        in_specs=[VMEM] * 11,
+        out_specs=(VMEM,) * 4,
+        compiler_params=limit,
+        name="grads_and_partial",
+    )(first, near, far, *local)
+    got = lax.ppermute(send, "core", [(0, 1), (1, 0)])
+    d_page, d_query, keep = pl.pallas_call(
+        page_kernel,
+        out_shape=(
+            jax.ShapeDtypeStruct((patches, per_dev, width), F32),
+            jax.ShapeDtypeStruct(d_query.shape, F32),
             jax.ShapeDtypeStruct((groups, share, width), F32),
         ),
-        in_specs=[VMEM] * 12,
-        out_specs=(VMEM,) * 4,
-        compiler_params=limit,
-        name="grads_and_partial",
-    )(first, near, far, *local, query_hidden)
-    got = lax.ppermute(send, "core", [(0, 1), (1, 0)])
-    d_page, keep = pl.pallas_call(
-        page_kernel,
-        out_shape=(jax.ShapeDtypeStruct((patches, per_dev, width), F32), jax.ShapeDtypeStruct(keep.shape, F32)),
-        in_specs=[VMEM] * 4 + [ANY],
-        out_specs=(VMEM, ANY),
-        input_output_aliases={4: 1},
+        in_specs=[VMEM] * 7,
+        out_specs=(ANY, ANY, VMEM),
+        scratch_shapes=[pltpu.VMEM((patches, per_dev, width), F32), pltpu.SemaphoreType.DMA((2,))],
         compiler_params=limit,
         cost_estimate=pl.CostEstimate(flops=10**9, bytes_accessed=10**6, transcendentals=0),
         name="page_grads",
-    )(values, table, unit, inv, keep)
+    )(values, low, here, table, unit, inv, d_query)
     small = pltpu.CompilerParams(vmem_limit_bytes=16 * 2**20)
     pair = pl.pallas_call(
         add_kernel,
@@ -330,7 +358,7 @@
         compiler_params=small,
         name="add_pair",
     )(keep, got)
-    parts = lax.all_to_all(pair.reshape(groups * 2, share // 2, width), ("blk", "mp"), 0, 0, tiled=True)
+    parts = lax.all_to_all(pair.reshape(groups * 2, share // 2, width), ("z0", "z1", "z2", "run", "mp"), 0, 0, tiled=True)
     grad = pl.pallas_call(
         sum_kernel,
         out_shape=jax.ShapeDtypeStruct((share // 2, width), F32),
@@ -344,20 +372,19 @@
 
 def solution(mesh):
     blocks, parts = mesh.devices.shape
-    fine = Mesh(mesh.devices.reshape(blocks // 2, 2, parts), ("blk", "core", "mp"))
-    dp = ("blk", "core")
+    fine = Mesh(mesh.devices.reshape(2, 2, 2, blocks // 16, 2, parts), DP + ("mp",))
     placed = (
-        P(dp, "mp", None),
-        P(dp, "mp", None),
-        P(dp, None, None),
-        P(dp, None, None),
-        P(dp, None, None),
-        P(dp),
+        P(DP, "mp", None),
+        P(DP, "mp", None),
+        P(DP, None, None),
+        P(DP, None, None),
+        P(DP, None, None),
+        P(DP),
     )
     return jax.shard_map(
         shards,
         mesh=fine,
         in_specs=placed,
-        out_specs=(P(dp, "mp", None), P(dp, "mp", None), P(("blk", "core", "mp"), None)),
+        out_specs=(P(DP, "mp", None), P(DP, "mp", None), P(DP + ("mp",), None)),
         check_vma=False,
     )

time: 42.9 us -> 41.7 us (0.972)
  blocking collectives: 28.9 us -> 28 us
  waiting for transfers between devices: 1.7 us -> 0.86 us
  Pallas kernels: 6.1 us -> 6.57 us
    all_to_all x1, blocking collectives: 28.9 us -> 28 us  [shards(): lax.all_to_all(pair.reshape(groups * 2, share // 2, width), ('z0', 'z1',...]
    pallas_call x1, Pallas kernels: 2.15 us -> 2.85 us  [shards(): pl.pallas_call(local_kernel, out_shape=(wide_rows, wide_rows, jax.ShapeDt...]
    ppermute x2, waiting for transfers between devices: 1.43 us -> 0.73 us  [the longest x1 0.72 us: shards(): far = lax.ppermute(second, DP + ('mp',), cross)]
  transfers between devices with their start and end apart: 3 -> 3, of which waited for: 2 -> 2; matrix products, arithmetic and copies ran while one was open for 0% -> 0% of each run, Pallas kernels for 8% -> 10%
where the time goes in v3:
time: 41.7 us; the launch traced here: 41.6 us
  blocking collectives  28 us (67%)
  Pallas kernels  6.57 us (16%)
  starting transfers between devices  4.38 us (11%)
  local copies, waits for them, and re-layouts  1.02 us (2%)
  waiting for transfers between devices  0.86 us (2%)
  between operations  0.74 us (2%)
    all_to_all x1, blocking collectives, shards(): lax.all_to_all(pair.reshape(groups * 2, share // 2, width), ('z0', 'z1',...  28 us
    ppermute x1, starting transfers between devices, shards(): far = lax.ppermute(second, DP + ('mp',), cross)  4.28 us
    pallas_call x1, Pallas kernels, shards(): pl.pallas_call(local_kernel, out_shape=(wide_rows, wide_rows, jax.ShapeDt...  2.85 us
    pallas_call x1, Pallas kernels, shards(): pl.pallas_call(page_kernel, out_shape=(jax.ShapeDtypeStruct((patches, per...  1.38 us
    unnamed x12, local copies, waits for them, and re-layouts  1.02 us
    pallas_call x1, Pallas kernels, shards(): pl.pallas_call(functools.partial(main_kernel, pages, per_dev), out_shape=...  0.99 us
  transfers between devices with their start and end apart: 3, of which 2 were waited for; matrix products, arithmetic and copies ran while one was open for 0% of the time, Pallas kernels for 10%

profile of v3, /device:TPU:32, one launch (start us, length us, event | category | flops | bytes accessed | tf_op | source)
XLA Modules:
  0.0 41.6 jit_solution(8842404023923341788)
XLA Ops:
  0.6 0.0 copy-start.3
  0.6 0.0 copy-start.2
  0.7 0.0 copy-start.1
  0.7 0.0 copy-start
  0.7 0.0 copy-start.5
  0.7 0.0 copy-start.4
  0.7 0.6 %copy-done.3 = s32[2]{0:T(128)S(1)} copy-done((s32[2]{0:T(128)S(1)}, s32[2]{0:T(128)}, u32[]{:S(2)}) %copy-start.3) | copy-done | bytes 32
  1.3 0.0 copy-done.2
  1.3 0.1 copy-done.1
  1.4 0.3 copy-done
  1.7 0.6 %gather_rows.1 = (bf16[208,128]{1,0:T(8,128)(2,1)S(1)}, bf16[208,128]{1,0:T(8,128)(2,1)S(1)}, bf16[256,128]{1,0:T(8,128)(2,1)S(1)}, bf16[515,2,128]{2,1,0:T(2,128)(2,1)S(1)}, s32[8,256]{1,0:T(8,128)S(1)}) custom-call(s32[8,128]{1,0:T(8,128)S(1)} %place.1.place_ref, s32[2,2,64]{2,1,0:T(2,128)S(1)} %copy-done.2, s32[1,2]{1,0:T(1,128)S(1)} %bitcast.9, ...), custom_call_target="tpu_custom_call" | custom-call | tf_op jit(solution)/shard_map/gather_rows/pallas_call | solution.py:273
  2.3 4.3 %collective-permute-start.1 = (bf16[208,128]{1,0:T(8,128)(2,1)S(1)}, bf16[208,128]{1,0:T(8,128)(2,1)S(1)}, u32[]{:S(2)}, u32[]{:S(2)}) collective-permute-start(bf16[208,128]{1,0:T(8,128)(2,1)S(1)} %get-tuple-element.28), channel_id=1, source_target_pairs={{0,255},{1,254},{2,4},{3,5},{4,2},{5,3},{6,8},{7,9},{8,6},{9,7},{1... | collective-permute-start | bytes 159752 | tf_op jit(solution)/shard_map/ppermute | solution.py:293
  6.6 0.0 collective-permute-start
  6.6 0.0 copy-done.5
  6.6 0.0 copy-done.4
  6.6 2.8 %local_rows.1 = (f32[1030,128]{1,0:T(8,128)S(1)}, f32[1030,128]{1,0:T(8,128)S(1)}, bf16[1030,256]{1,0:T(8,128)(2,1)S(1)}, f32[128,128]{1,0:T(8,128)S(1)}, f32[12...) custom-call(bf16[208,128]{1,0:T(8,128)(2,1)S(1)} %get-tuple-element., ...), custom_call_target="tpu_custom_call" | custom-call | flops 5000000000 | bytes 1000000 | tf_op jit(solution)/shard_map/local_rows/pallas_call | solution.py:302
  9.5 0.7 %collective-permute-done.1.second_ref = bf16[208,128]{1,0:T(8,128)(2,1)S(1)} collective-permute-done((bf16[208,128]{1,0:T(8,128)(2,1)S(1)}, bf16[208,128]{1,0:T(8,128)(2,1)S(1)}, u32[]{:S(2)}, u32[]{:S(2)}) %collective-permute-start.1) | collective-permute-done | bytes 53280 | tf_op jit(solution)/shard_map/ppermute | solution.py:293
  10.2 0.0 collective-permute-done.first_ref
  10.2 1.0 %grads_and_partial.1 = (f32[2,16,128]{2,1,0:T(8,128)S(1)}, bf16[256,256]{1,0:T(8,128)(2,1)S(1)}, bf16[288,128]{1,0:T(8,128)(2,1)S(1)}, bf16[64,16,128]{2,1,0:T(8,128)(2,1)S(1)}) custom-call(bf16[208,128]{1,0:T(8,128)(2,1)S(1)} %get-tuple-element.27.sent_ref, bf16[208,128]{1,0:T(8,128)(2,1)S(1)} %collective-permute-done.first_ref, ...), custom_call_target="tpu_custom_call" | custom-call | tf_op jit(solution)/shard_map/grads_and_partial/pallas_call | solution.py:324
  11.2 0.1 collective-permute-start.2
  11.3 1.4 %page_grads.1 = (f32[515,2,128]{2,1,0:T(2,128)}, f32[2,16,128]{2,1,0:T(8,128)}, f32[64,16,128]{2,1,0:T(8,128)S(1)}) custom-call(bf16[256,256]{1,0:T(8,128)(2,1)S(1)} %get-tuple-element.40.values_ref, bf16[288,128]{1,0:T(8,128)(2,1)S(1)} %get-tuple-element.41.low_ref, bf16[64,16,288]{2,1,0:T(8,128)(2,1)S(1)} %get-tuple-element.42.here_ref, ...), custom_call_target="tpu_custom_call" | custom-call | flops 1000000000 | bytes 1000000 | tf_op jit(solution)/shard_map/page_grads/pallas_call | solution.py:338
  12.7 0.1 collective-permute-done.2.got_ref
  12.9 28.0 %all_to_all.5 = bf16[128,8,128]{2,1,0:T(8,128)(2,1)S(1)} all-to-all(bf16[128,8,128]{2,1,0:T(8,128)(2,1)S(1)} %bitcast.7), channel_id=1, replica_groups=mesh['z2'=2,'z1'=2,'z0'=2,'run'=8,'core'=2,'mp'=2] {'z0','z1','z2','run'..., dimensions={0} | all-to-all | bytes 524288 | tf_op jit(solution)/shard_map/all_to_all | solution.py:361
  40.9 0.7 %sum_parts.1 = f32[8,128]{1,0:T(8,128)} custom-call(bf16[64,16,128]{2,1,0:T(8,128)(2,1)S(1)} %bitcast.6), custom_call_target="tpu_custom_call" | custom-call | tf_op jit(solution)/shard_map/sum_parts/pallas_call | solution.py:362
  (2 shorter events, 0.1 us)
Async XLA Ops:
  0.6 0.7 %copy-start.3 = (s32[2]{0:T(128)S(1)}, s32[2]{0:T(128)}, u32[]{:S(2)}) copy-start(s32[2]{0:T(128)} %param.11) | copy-start | bytes 28
  0.6 0.7 %copy-start.2 = (s32[2,2,64]{2,1,0:T(2,128)S(1)}, s32[2,2,64]{2,1,0:T(2,128)}, u32[]{:S(2)}) copy-start(s32[2,2,64]{2,1,0:T(2,128)} %idx_ref.1) | copy-start | bytes 3076
  0.7 0.7 %copy-start.1 = (bf16[2,32,128]{2,1,0:T(8,128)(2,1)S(1)}, bf16[2,32,128]{2,1,0:T(8,128)(2,1)}, u32[]{:S(2)}) copy-start(bf16[2,32,128]{2,1,0:T(8,128)(2,1)} %query_ref.1) | copy-start | bytes 49156
  0.7 1.1 %copy-start = (bf16[2,1030,128]{2,0,1:T(2,128)(2,1)S(1)}, bf16[2,1030,128]{2,0,1:T(2,128)(2,1)}, u32[]{:S(2)}) copy-start(bf16[2,1030,128]{2,0,1:T(2,128)(2,1)} %param.8) | copy-start | bytes 1582084
  0.7 6.0 %copy-start.5 = (bf16[2,16,2048]{2,1,0:T(8,128)(2,1)S(1)}, bf16[2,16,2048]{2,1,0:T(8,128)(2,1)}, u32[]{:S(2)}) copy-start(bf16[2,16,2048]{2,1,0:T(8,128)(2,1)} %qhid_ref.1) | copy-start | bytes 393220
  0.7 6.0 %copy-start.4 = (bf16[2,515,2048]{2,0,1:T(2,128)(2,1)S(1)}, bf16[2,515,2048]{2,0,1:T(2,128)(2,1)}, u32[]{:S(2)}) copy-start(bf16[2,515,2048]{2,0,1:T(2,128)(2,1)} %param.6) | copy-start | bytes 12656644
  2.3 7.9 %collective-permute-start.1 = (bf16[208,128]{1,0:T(8,128)(2,1)S(1)}, bf16[208,128]{1,0:T(8,128)(2,1)S(1)}, u32[]{:S(2)}, u32[]{:S(2)}) collective-permute-start(bf16[208,128]{1,0:T(8,128)(2,1)S(1)} %get-tuple-element.28), channel_id=1, source_target_pairs={{0,255},{1,254},{2,4},{3,5},{4,2},{5,3},{6,8},{7,9},{8,6},{9,7},{1... | collective-permute-start | bytes 159752 | tf_op jit(solution)/shard_map/ppermute | solution.py:293
  6.6 3.6 %collective-permute-start = (bf16[208,128]{1,0:T(8,128)(2,1)S(1)}, bf16[208,128]{1,0:T(8,128)(2,1)S(1)}, u32[]{:S(2)}, u32[]{:S(2)}) collective-permute-start(bf16[208,128]{1,0:T(8,128)(2,1)S(1)} %get-tuple-element.27.sent_ref), channel_id=1, source_target_pairs={{0,2},{2,0},{4,6},{6,4},{8,10},{10,8},{12,14},{14,12},{16,18},{18,... | collective-permute-start | bytes 159752 | tf_op jit(solution)/shard_map/ppermute | solution.py:294
  11.2 1.6 %collective-permute-start.2 = (bf16[64,16,128]{2,1,0:T(8,128)(2,1)S(1)}, bf16[64,16,128]{2,1,0:T(8,128)(2,1)S(1)}, u32[]{:S(2)}, u32[]{:S(2)}) collective-permute-start(bf16[64,16,128]{2,1,0:T(8,128)(2,1)S(1)} %get-tuple-element.50), channel_id=1, source_target_pairs={{0,2},{2,0},{1,3},{3,1},{4,6},{6,4},{5,7},{7,5},{8,10},{10,8},{9,1... | collective-permute-start | bytes 786440 | tf_op jit(solution)/shard_map/ppermute | solution.py:337

commit v4 on v3

--- a/solution.py
+++ b/solution.py
@@ -16,8 +16,23 @@
 PLANES = 8
 BLK = ("z2", "z1", "z0", "run")
 DP = BLK + ("core",)
+RUNS = 8
+ORDER = ("z0", "z1", "z2", "x0", "x1", "yh", "mp")
 VMEM = pl.BlockSpec(memory_space=pltpu.VMEM)
 ANY = pl.BlockSpec(memory_space=pl.ANY)
+
+
+def exchange_order():
+    names = ("z2", "z1", "z0", "yh", "x1", "x0", "core", "mp")
+    members, places = ([], []), [0] * (PLANES * RUNS)
+    for place in range(2 ** len(ORDER)):
+        bits = {name: 1 - (place >> (len(ORDER) - 1 - i)) % 2 for i, name in enumerate(ORDER)}
+        for core in range(2):
+            bits["core"] = core
+            device = functools.reduce(lambda total, name: total * 2 + bits[name], names, 0)
+            members[core].append(device)
+        places[device // 4] = place // 2
+    return members, places
 
 
 def one_hot(targets, rows):
@@ -235,11 +250,10 @@
 
 
 def add_kernel(keep_ref, got_ref, out_ref):
-    size = keep_ref.shape[0] // PLANES
-    for z in range(PLANES):
-        at = ((z & 1) * 4 + (z & 2) + (z >> 2)) * size
-        here = slice(z * size, (z + 1) * size)
-        out_ref[at : at + size] = (keep_ref[here] + got_ref[here].astype(F32)).astype(BF16)
+    rows = keep_ref.shape[1] // 2
+    for group, place in enumerate(exchange_order()[1]):
+        total = keep_ref[group] + got_ref[group].astype(F32)
+        out_ref[place] = jnp.concatenate([total[rows:], total[:rows]], axis=0).astype(BF16)
 
 
 def sum_kernel(parts_ref, out_ref):
@@ -358,7 +372,14 @@
         compiler_params=small,
         name="add_pair",
     )(keep, got)
-    parts = lax.all_to_all(pair.reshape(groups * 2, share // 2, width), ("z0", "z1", "z2", "run", "mp"), 0, 0, tiled=True)
+    parts = lax.all_to_all(
+        pair.reshape(groups * 2, share // 2, width),
+        DP + ("mp",),
+        0,
+        0,
+        tiled=True,
+        axis_index_groups=exchange_order()[0],
+    )
     grad = pl.pallas_call(
         sum_kernel,
         out_shape=jax.ShapeDtypeStruct((share // 2, width), F32),

time: 41.7 us -> 38.5 us (0.923)
  blocking collectives: 28 us -> 24.8 us
    all_to_all x1, blocking collectives: 28 us -> 24.8 us  [shards(): lax.all_to_all(pair.reshape(groups * 2, share // 2, width), DP + ('mp',),...]
  transfers between devices with their start and end apart: 3 -> 3, of which waited for: 2 -> 2; matrix products, arithmetic and copies ran while one was open for 0% -> 0% of each run, Pallas kernels for 10% -> 11%
where the time goes in v4:
time: 38.5 us; the launch traced here: 38.4 us
  blocking collectives  24.8 us (64%)
  Pallas kernels  6.57 us (17%)
  starting transfers between devices  4.38 us (11%)
  local copies, waits for them, and re-layouts  1.02 us (3%)
  waiting for transfers between devices  0.86 us (2%)
  between operations  0.74 us (2%)
    all_to_all x1, blocking collectives, shards(): lax.all_to_all(pair.reshape(groups * 2, share // 2, width), DP + ('mp',),...  24.8 us
    ppermute x1, starting transfers between devices, shards(): far = lax.ppermute(second, DP + ('mp',), cross)  4.28 us
    pallas_call x1, Pallas kernels, shards(): pl.pallas_call(local_kernel, out_shape=(wide_rows, wide_rows, jax.ShapeDt...  2.85 us
    pallas_call x1, Pallas kernels, shards(): pl.pallas_call(page_kernel, out_shape=(jax.ShapeDtypeStruct((patches, per...  1.38 us
    unnamed x12, local copies, waits for them, and re-layouts  1.02 us
    pallas_call x1, Pallas kernels, shards(): pl.pallas_call(functools.partial(main_kernel, pages, per_dev), out_shape=...  0.99 us
  transfers between devices with their start and end apart: 3, of which 2 were waited for; matrix products, arithmetic and copies ran while one was open for 0% of the time, Pallas kernels for 11%

profile of v4, /device:TPU:32, one launch (start us, length us, event | category | flops | bytes accessed | tf_op | source)
XLA Modules:
  0.0 38.4 jit_solution(13959870993065010450)
XLA Ops:
  0.6 0.0 copy-start.3
  0.6 0.0 copy-start.2
  0.7 0.0 copy-start.1
  0.7 0.0 copy-start
  0.7 0.0 copy-start.5
  0.7 0.0 copy-start.4
  0.7 0.6 %copy-done.3 = s32[2]{0:T(128)S(1)} copy-done((s32[2]{0:T(128)S(1)}, s32[2]{0:T(128)}, u32[]{:S(2)}) %copy-start.3) | copy-done | bytes 32
  1.3 0.0 copy-done.2
  1.3 0.1 copy-done.1
  1.4 0.3 copy-done
  1.7 0.6 %gather_rows.1 = (bf16[208,128]{1,0:T(8,128)(2,1)S(1)}, bf16[208,128]{1,0:T(8,128)(2,1)S(1)}, bf16[256,128]{1,0:T(8,128)(2,1)S(1)}, bf16[515,2,128]{2,1,0:T(2,128)(2,1)S(1)}, s32[8,256]{1,0:T(8,128)S(1)}) custom-call(s32[8,128]{1,0:T(8,128)S(1)} %place.1.place_ref, s32[2,2,64]{2,1,0:T(2,128)S(1)} %copy-done.2, s32[1,2]{1,0:T(1,128)S(1)} %bitcast.9, ...), custom_call_target="tpu_custom_call" | custom-call | tf_op jit(solution)/shard_map/gather_rows/pallas_call | solution.py:287
  2.3 4.3 %collective-permute-start.1 = (bf16[208,128]{1,0:T(8,128)(2,1)S(1)}, bf16[208,128]{1,0:T(8,128)(2,1)S(1)}, u32[]{:S(2)}, u32[]{:S(2)}) collective-permute-start(bf16[208,128]{1,0:T(8,128)(2,1)S(1)} %get-tuple-element.28), channel_id=1, source_target_pairs={{0,255},{1,254},{2,4},{3,5},{4,2},{5,3},{6,8},{7,9},{8,6},{9,7},{1... | collective-permute-start | bytes 159752 | tf_op jit(solution)/shard_map/ppermute | solution.py:307
  6.6 0.0 collective-permute-start
  6.6 0.0 copy-done.5
  6.6 0.0 copy-done.4
  6.6 2.8 %local_rows.1 = (f32[1030,128]{1,0:T(8,128)S(1)}, f32[1030,128]{1,0:T(8,128)S(1)}, bf16[1030,256]{1,0:T(8,128)(2,1)S(1)}, f32[128,128]{1,0:T(8,128)S(1)}, f32[12...) custom-call(bf16[208,128]{1,0:T(8,128)(2,1)S(1)} %get-tuple-element., ...), custom_call_target="tpu_custom_call" | custom-call | flops 5000000000 | bytes 1000000 | tf_op jit(solution)/shard_map/local_rows/pallas_call | solution.py:316
  9.5 0.7 %collective-permute-done.1.second_ref = bf16[208,128]{1,0:T(8,128)(2,1)S(1)} collective-permute-done((bf16[208,128]{1,0:T(8,128)(2,1)S(1)}, bf16[208,128]{1,0:T(8,128)(2,1)S(1)}, u32[]{:S(2)}, u32[]{:S(2)}) %collective-permute-start.1) | collective-permute-done | bytes 53280 | tf_op jit(solution)/shard_map/ppermute | solution.py:307
  10.2 0.0 collective-permute-done.first_ref
  10.2 1.0 %grads_and_partial.1 = (f32[2,16,128]{2,1,0:T(8,128)S(1)}, bf16[256,256]{1,0:T(8,128)(2,1)S(1)}, bf16[288,128]{1,0:T(8,128)(2,1)S(1)}, bf16[64,16,128]{2,1,0:T(8,128)(2,1)S(1)}) custom-call(bf16[208,128]{1,0:T(8,128)(2,1)S(1)} %get-tuple-element.27.sent_ref, bf16[208,128]{1,0:T(8,128)(2,1)S(1)} %collective-permute-done.first_ref, ...), custom_call_target="tpu_custom_call" | custom-call | tf_op jit(solution)/shard_map/grads_and_partial/pallas_call | solution.py:338
  11.2 0.1 collective-permute-start.2
  11.3 1.4 %page_grads.1 = (f32[515,2,128]{2,1,0:T(2,128)}, f32[2,16,128]{2,1,0:T(8,128)}, f32[64,16,128]{2,1,0:T(8,128)S(1)}) custom-call(bf16[256,256]{1,0:T(8,128)(2,1)S(1)} %get-tuple-element.40.values_ref, bf16[288,128]{1,0:T(8,128)(2,1)S(1)} %get-tuple-element.41.low_ref, bf16[64,16,288]{2,1,0:T(8,128)(2,1)S(1)} %get-tuple-element.42.here_ref, ...), custom_call_target="tpu_custom_call" | custom-call | flops 1000000000 | bytes 1000000 | tf_op jit(solution)/shard_map/page_grads/pallas_call | solution.py:352
  12.7 0.1 collective-permute-done.2.got_ref
  12.9 24.8 %all_to_all.5 = bf16[128,8,128]{2,1,0:T(8,128)(2,1)S(1)} all-to-all(bf16[128,8,128]{2,1,0:T(8,128)(2,1)S(1)} %bitcast.7), channel_id=1, replica_groups={{253,252,237,236,245,244,229,228,249,248,233,232,241,240,225,224,125,12..., dimensions={0} | all-to-all | bytes 524288 | tf_op jit(solution)/shard_map/all_to_all | solution.py:375
  37.7 0.7 %sum_parts.1 = f32[8,128]{1,0:T(8,128)} custom-call(bf16[64,16,128]{2,1,0:T(8,128)(2,1)S(1)} %bitcast.6), custom_call_target="tpu_custom_call" | custom-call | tf_op jit(solution)/shard_map/sum_parts/pallas_call | solution.py:383
  (2 shorter events, 0.1 us)
Async XLA Ops:
  0.6 0.7 %copy-start.3 = (s32[2]{0:T(128)S(1)}, s32[2]{0:T(128)}, u32[]{:S(2)}) copy-start(s32[2]{0:T(128)} %param.11) | copy-start | bytes 28
  0.6 0.7 %copy-start.2 = (s32[2,2,64]{2,1,0:T(2,128)S(1)}, s32[2,2,64]{2,1,0:T(2,128)}, u32[]{:S(2)}) copy-start(s32[2,2,64]{2,1,0:T(2,128)} %idx_ref.1) | copy-start | bytes 3076
  0.7 0.7 %copy-start.1 = (bf16[2,32,128]{2,1,0:T(8,128)(2,1)S(1)}, bf16[2,32,128]{2,1,0:T(8,128)(2,1)}, u32[]{:S(2)}) copy-start(bf16[2,32,128]{2,1,0:T(8,128)(2,1)} %query_ref.1) | copy-start | bytes 49156
  0.7 1.1 %copy-start = (bf16[2,1030,128]{2,0,1:T(2,128)(2,1)S(1)}, bf16[2,1030,128]{2,0,1:T(2,128)(2,1)}, u32[]{:S(2)}) copy-start(bf16[2,1030,128]{2,0,1:T(2,128)(2,1)} %param.8) | copy-start | bytes 1582084
  0.7 6.0 %copy-start.5 = (bf16[2,16,2048]{2,1,0:T(8,128)(2,1)S(1)}, bf16[2,16,2048]{2,1,0:T(8,128)(2,1)}, u32[]{:S(2)}) copy-start(bf16[2,16,2048]{2,1,0:T(8,128)(2,1)} %qhid_ref.1) | copy-start | bytes 393220
  0.7 6.0 %copy-start.4 = (bf16[2,515,2048]{2,0,1:T(2,128)(2,1)S(1)}, bf16[2,515,2048]{2,0,1:T(2,128)(2,1)}, u32[]{:S(2)}) copy-start(bf16[2,515,2048]{2,0,1:T(2,128)(2,1)} %param.6) | copy-start | bytes 12656644
  2.3 7.9 %collective-permute-start.1 = (bf16[208,128]{1,0:T(8,128)(2,1)S(1)}, bf16[208,128]{1,0:T(8,128)(2,1)S(1)}, u32[]{:S(2)}, u32[]{:S(2)}) collective-permute-start(bf16[208,128]{1,0:T(8,128)(2,1)S(1)} %get-tuple-element.28), channel_id=1, source_target_pairs={{0,255},{1,254},{2,4},{3,5},{4,2},{5,3},{6,8},{7,9},{8,6},{9,7},{1... | collective-permute-start | bytes 159752 | tf_op jit(solution)/shard_map/ppermute | solution.py:307
  6.6 3.6 %collective-permute-start = (bf16[208,128]{1,0:T(8,128)(2,1)S(1)}, bf16[208,128]{1,0:T(8,128)(2,1)S(1)}, u32[]{:S(2)}, u32[]{:S(2)}) collective-permute-start(bf16[208,128]{1,0:T(8,128)(2,1)S(1)} %get-tuple-element.27.sent_ref), channel_id=1, source_target_pairs={{0,2},{2,0},{4,6},{6,4},{8,10},{10,8},{12,14},{14,12},{16,18},{18,... | collective-permute-start | bytes 159752 | tf_op jit(solution)/shard_map/ppermute | solution.py:308
  11.2 1.6 %collective-permute-start.2 = (bf16[64,16,128]{2,1,0:T(8,128)(2,1)S(1)}, bf16[64,16,128]{2,1,0:T(8,128)(2,1)S(1)}, u32[]{:S(2)}, u32[]{:S(2)}) collective-permute-start(bf16[64,16,128]{2,1,0:T(8,128)(2,1)S(1)} %get-tuple-element.50), channel_id=1, source_target_pairs={{0,2},{2,0},{1,3},{3,1},{4,6},{6,4},{5,7},{7,5},{8,10},{10,8},{9,1... | collective-permute-start | bytes 786440 | tf_op jit(solution)/shard_map/ppermute | solution.py:351

commit v5 on v4

--- a/solution.py
+++ b/solution.py
@@ -26,7 +26,8 @@
     names = ("z2", "z1", "z0", "yh", "x1", "x0", "core", "mp")
     members, places = ([], []), [0] * (PLANES * RUNS)
     for place in range(2 ** len(ORDER)):
-        bits = {name: 1 - (place >> (len(ORDER) - 1 - i)) % 2 for i, name in enumerate(ORDER)}
+        bits = {name: (place >> (len(ORDER) - 1 - i)) % 2 for i, name in enumerate(ORDER)}
+        bits = {name: bit if name == "mp" else 1 - bit for name, bit in bits.items()}
         for core in range(2):
             bits["core"] = core
             device = functools.reduce(lambda total, name: total * 2 + bits[name], names, 0)
@@ -250,10 +251,8 @@
 
 
 def add_kernel(keep_ref, got_ref, out_ref):
-    rows = keep_ref.shape[1] // 2
     for group, place in enumerate(exchange_order()[1]):
-        total = keep_ref[group] + got_ref[group].astype(F32)
-        out_ref[place] = jnp.concatenate([total[rows:], total[:rows]], axis=0).astype(BF16)
+        out_ref[place] = (keep_ref[group] + got_ref[group].astype(F32)).astype(BF16)
 
 
 def sum_kernel(parts_ref, out_ref):

time: 38.5 us -> 38 us (0.987); the launches traced: 38.4 us -> 37.4 us
  blocking collectives: 24.8 us -> 23.8 us
    all_to_all x1, blocking collectives: 24.8 us -> 23.8 us  [shards(): lax.all_to_all(pair.reshape(groups * 2, share // 2, width), DP + ('mp',),...]
where the time goes in v5:
time: 38 us; the launch traced here: 37.4 us
  blocking collectives  23.8 us (63%)
  Pallas kernels  6.57 us (17%)
  starting transfers between devices  4.38 us (12%)
  local copies, waits for them, and re-layouts  1.02 us (3%)
  waiting for transfers between devices  0.86 us (2%)
  between operations  0.74 us (2%)
    all_to_all x1, blocking collectives, shards(): lax.all_to_all(pair.reshape(groups * 2, share // 2, width), DP + ('mp',),...  23.8 us
    ppermute x1, starting transfers between devices, shards(): far = lax.ppermute(second, DP + ('mp',), cross)  4.28 us
    pallas_call x1, Pallas kernels, shards(): pl.pallas_call(local_kernel, out_shape=(wide_rows, wide_rows, jax.ShapeDt...  2.85 us
    pallas_call x1, Pallas kernels, shards(): pl.pallas_call(page_kernel, out_shape=(jax.ShapeDtypeStruct((patches, per...  1.38 us
    unnamed x12, local copies, waits for them, and re-layouts  1.02 us
    pallas_call x1, Pallas kernels, shards(): pl.pallas_call(functools.partial(main_kernel, pages, per_dev), out_shape=...  0.99 us
  transfers between devices with their start and end apart: 3, of which 2 were waited for; matrix products, arithmetic and copies ran while one was open for 0% of the time, Pallas kernels for 11%

profile of v5, /device:TPU:32, one launch (start us, length us, event | category | flops | bytes accessed | tf_op | source)
XLA Modules:
  0.0 37.4 jit_solution(2953658334989170739)
XLA Ops:
  0.6 0.0 copy-start.3
  0.6 0.0 copy-start.2
  0.7 0.0 copy-start.1
  0.7 0.0 copy-start
  0.7 0.0 copy-start.5
  0.7 0.0 copy-start.4
  0.7 0.6 %copy-done.3 = s32[2]{0:T(128)S(1)} copy-done((s32[2]{0:T(128)S(1)}, s32[2]{0:T(128)}, u32[]{:S(2)}) %copy-start.3) | copy-done | bytes 32
  1.3 0.0 copy-done.2
  1.3 0.1 copy-done.1
  1.4 0.3 copy-done
  1.7 0.6 %gather_rows.1 = (bf16[208,128]{1,0:T(8,128)(2,1)S(1)}, bf16[208,128]{1,0:T(8,128)(2,1)S(1)}, bf16[256,128]{1,0:T(8,128)(2,1)S(1)}, bf16[515,2,128]{2,1,0:T(2,128)(2,1)S(1)}, s32[8,256]{1,0:T(8,128)S(1)}) custom-call(s32[8,128]{1,0:T(8,128)S(1)} %place.1.place_ref, s32[2,2,64]{2,1,0:T(2,128)S(1)} %copy-done.2, s32[1,2]{1,0:T(1,128)S(1)} %bitcast.9, ...), custom_call_target="tpu_custom_call" | custom-call | tf_op jit(solution)/shard_map/gather_rows/pallas_call | solution.py:286
  2.3 4.3 %collective-permute-start.1 = (bf16[208,128]{1,0:T(8,128)(2,1)S(1)}, bf16[208,128]{1,0:T(8,128)(2,1)S(1)}, u32[]{:S(2)}, u32[]{:S(2)}) collective-permute-start(bf16[208,128]{1,0:T(8,128)(2,1)S(1)} %get-tuple-element.28), channel_id=1, source_target_pairs={{0,255},{1,254},{2,4},{3,5},{4,2},{5,3},{6,8},{7,9},{8,6},{9,7},{1... | collective-permute-start | bytes 159752 | tf_op jit(solution)/shard_map/ppermute | solution.py:306
  6.6 0.0 collective-permute-start
  6.6 0.0 copy-done.5
  6.6 0.0 copy-done.4
  6.6 2.8 %local_rows.1 = (f32[1030,128]{1,0:T(8,128)S(1)}, f32[1030,128]{1,0:T(8,128)S(1)}, bf16[1030,256]{1,0:T(8,128)(2,1)S(1)}, f32[128,128]{1,0:T(8,128)S(1)}, f32[12...) custom-call(bf16[208,128]{1,0:T(8,128)(2,1)S(1)} %get-tuple-element., ...), custom_call_target="tpu_custom_call" | custom-call | flops 5000000000 | bytes 1000000 | tf_op jit(solution)/shard_map/local_rows/pallas_call | solution.py:315
  9.5 0.7 %collective-permute-done.1.second_ref = bf16[208,128]{1,0:T(8,128)(2,1)S(1)} collective-permute-done((bf16[208,128]{1,0:T(8,128)(2,1)S(1)}, bf16[208,128]{1,0:T(8,128)(2,1)S(1)}, u32[]{:S(2)}, u32[]{:S(2)}) %collective-permute-start.1) | collective-permute-done | bytes 53280 | tf_op jit(solution)/shard_map/ppermute | solution.py:306
  10.2 0.0 collective-permute-done.first_ref
  10.2 1.0 %grads_and_partial.1 = (f32[2,16,128]{2,1,0:T(8,128)S(1)}, bf16[256,256]{1,0:T(8,128)(2,1)S(1)}, bf16[288,128]{1,0:T(8,128)(2,1)S(1)}, bf16[64,16,128]{2,1,0:T(8,128)(2,1)S(1)}) custom-call(bf16[208,128]{1,0:T(8,128)(2,1)S(1)} %get-tuple-element.27.sent_ref, bf16[208,128]{1,0:T(8,128)(2,1)S(1)} %collective-permute-done.first_ref, ...), custom_call_target="tpu_custom_call" | custom-call | tf_op jit(solution)/shard_map/grads_and_partial/pallas_call | solution.py:337
  11.2 0.1 collective-permute-start.2
  11.3 1.4 %page_grads.1 = (f32[515,2,128]{2,1,0:T(2,128)}, f32[2,16,128]{2,1,0:T(8,128)}, f32[64,16,128]{2,1,0:T(8,128)S(1)}) custom-call(bf16[256,256]{1,0:T(8,128)(2,1)S(1)} %get-tuple-element.40.values_ref, bf16[288,128]{1,0:T(8,128)(2,1)S(1)} %get-tuple-element.41.low_ref, bf16[64,16,288]{2,1,0:T(8,128)(2,1)S(1)} %get-tuple-element.42.here_ref, ...), custom_call_target="tpu_custom_call" | custom-call | flops 1000000000 | bytes 1000000 | tf_op jit(solution)/shard_map/page_grads/pallas_call | solution.py:351
  12.7 0.1 collective-permute-done.2.got_ref
  12.9 23.8 %all_to_all.5 = bf16[128,8,128]{2,1,0:T(8,128)(2,1)S(1)} all-to-all(bf16[128,8,128]{2,1,0:T(8,128)(2,1)S(1)} %bitcast.7), channel_id=1, replica_groups={{252,253,236,237,244,245,228,229,248,249,232,233,240,241,224,225,124,12..., dimensions={0} | all-to-all | bytes 524288 | tf_op jit(solution)/shard_map/all_to_all | solution.py:374
  36.7 0.7 %sum_parts.1 = f32[8,128]{1,0:T(8,128)} custom-call(bf16[64,16,128]{2,1,0:T(8,128)(2,1)S(1)} %bitcast.6), custom_call_target="tpu_custom_call" | custom-call | tf_op jit(solution)/shard_map/sum_parts/pallas_call | solution.py:382
  (2 shorter events, 0.1 us)
Async XLA Ops:
  0.6 0.7 %copy-start.3 = (s32[2]{0:T(128)S(1)}, s32[2]{0:T(128)}, u32[]{:S(2)}) copy-start(s32[2]{0:T(128)} %param.11) | copy-start | bytes 28
  0.6 0.7 %copy-start.2 = (s32[2,2,64]{2,1,0:T(2,128)S(1)}, s32[2,2,64]{2,1,0:T(2,128)}, u32[]{:S(2)}) copy-start(s32[2,2,64]{2,1,0:T(2,128)} %idx_ref.1) | copy-start | bytes 3076
  0.7 0.7 %copy-start.1 = (bf16[2,32,128]{2,1,0:T(8,128)(2,1)S(1)}, bf16[2,32,128]{2,1,0:T(8,128)(2,1)}, u32[]{:S(2)}) copy-start(bf16[2,32,128]{2,1,0:T(8,128)(2,1)} %query_ref.1) | copy-start | bytes 49156
  0.7 1.1 %copy-start = (bf16[2,1030,128]{2,0,1:T(2,128)(2,1)S(1)}, bf16[2,1030,128]{2,0,1:T(2,128)(2,1)}, u32[]{:S(2)}) copy-start(bf16[2,1030,128]{2,0,1:T(2,128)(2,1)} %param.8) | copy-start | bytes 1582084
  0.7 6.0 %copy-start.5 = (bf16[2,16,2048]{2,1,0:T(8,128)(2,1)S(1)}, bf16[2,16,2048]{2,1,0:T(8,128)(2,1)}, u32[]{:S(2)}) copy-start(bf16[2,16,2048]{2,1,0:T(8,128)(2,1)} %qhid_ref.1) | copy-start | bytes 393220
  0.7 6.0 %copy-start.4 = (bf16[2,515,2048]{2,0,1:T(2,128)(2,1)S(1)}, bf16[2,515,2048]{2,0,1:T(2,128)(2,1)}, u32[]{:S(2)}) copy-start(bf16[2,515,2048]{2,0,1:T(2,128)(2,1)} %param.6) | copy-start | bytes 12656644
  2.3 7.9 %collective-permute-start.1 = (bf16[208,128]{1,0:T(8,128)(2,1)S(1)}, bf16[208,128]{1,0:T(8,128)(2,1)S(1)}, u32[]{:S(2)}, u32[]{:S(2)}) collective-permute-start(bf16[208,128]{1,0:T(8,128)(2,1)S(1)} %get-tuple-element.28), channel_id=1, source_target_pairs={{0,255},{1,254},{2,4},{3,5},{4,2},{5,3},{6,8},{7,9},{8,6},{9,7},{1... | collective-permute-start | bytes 159752 | tf_op jit(solution)/shard_map/ppermute | solution.py:306
  6.6 3.6 %collective-permute-start = (bf16[208,128]{1,0:T(8,128)(2,1)S(1)}, bf16[208,128]{1,0:T(8,128)(2,1)S(1)}, u32[]{:S(2)}, u32[]{:S(2)}) collective-permute-start(bf16[208,128]{1,0:T(8,128)(2,1)S(1)} %get-tuple-element.27.sent_ref), channel_id=1, source_target_pairs={{0,2},{2,0},{4,6},{6,4},{8,10},{10,8},{12,14},{14,12},{16,18},{18,... | collective-permute-start | bytes 159752 | tf_op jit(solution)/shard_map/ppermute | solution.py:307
  11.2 1.6 %collective-permute-start.2 = (bf16[64,16,128]{2,1,0:T(8,128)(2,1)S(1)}, bf16[64,16,128]{2,1,0:T(8,128)(2,1)S(1)}, u32[]{:S(2)}, u32[]{:S(2)}) collective-permute-start(bf16[64,16,128]{2,1,0:T(8,128)(2,1)S(1)} %get-tuple-element.50), channel_id=1, source_target_pairs={{0,2},{2,0},{1,3},{3,1},{4,6},{6,4},{5,7},{7,5},{8,10},{10,8},{9,1... | collective-permute-start | bytes 786440 | tf_op jit(solution)/shard_map/ppermute | solution.py:350

commit v6 on v5

--- a/solution.py
+++ b/solution.py
@@ -17,22 +17,22 @@
 BLK = ("z2", "z1", "z0", "run")
 DP = BLK + ("core",)
 RUNS = 8
-ORDER = ("z0", "z1", "z2", "x0", "x1", "yh", "mp")
+ORDERS = (("z0", "z1", "z2", "x0", "x1", "yh", "mp"), ("z0", "z1", "z2", "yh", "x1", "x0", "mp"))
 VMEM = pl.BlockSpec(memory_space=pltpu.VMEM)
 ANY = pl.BlockSpec(memory_space=pl.ANY)
 
 
 def exchange_order():
     names = ("z2", "z1", "z0", "yh", "x1", "x0", "core", "mp")
-    members, places = ([], []), [0] * (PLANES * RUNS)
-    for place in range(2 ** len(ORDER)):
-        bits = {name: (place >> (len(ORDER) - 1 - i)) % 2 for i, name in enumerate(ORDER)}
-        bits = {name: bit if name == "mp" else 1 - bit for name, bit in bits.items()}
-        for core in range(2):
+    members, places = ([], []), ([0] * (PLANES * RUNS), [0] * (PLANES * RUNS))
+    for core, order in enumerate(ORDERS):
+        for place in range(2 ** len(order)):
+            bits = {name: (place >> (len(order) - 1 - i)) % 2 for i, name in enumerate(order)}
+            bits = {name: bit if name == "mp" else 1 - bit for name, bit in bits.items()}
             bits["core"] = core
             device = functools.reduce(lambda total, name: total * 2 + bits[name], names, 0)
             members[core].append(device)
-        places[device // 4] = place // 2
+            places[core][device // 4] = place // 2
     return members, places
 
 
@@ -251,8 +251,12 @@
 
 
 def add_kernel(keep_ref, got_ref, out_ref):
-    for group, place in enumerate(exchange_order()[1]):
-        out_ref[place] = (keep_ref[group] + got_ref[group].astype(F32)).astype(BF16)
+    for core, places in enumerate(exchange_order()[1]):
+
+        @pl.when(lax.axis_index("core") == core)
+        def _(places=places):
+            for group, place in enumerate(places):
+                out_ref[place] = (keep_ref[group] + got_ref[group].astype(F32)).astype(BF16)
 
 
 def sum_kernel(parts_ref, out_ref):

time: 38 us -> 38.1 us (level)
  no operation moved by 1% of the time
where the time goes in v6:
time: 38.1 us; the launch traced here: 37.4 us
  blocking collectives  23.8 us (62%)
  Pallas kernels  6.57 us (17%)
  starting transfers between devices  4.38 us (11%)
  local copies, waits for them, and re-layouts  1.02 us (3%)
  waiting for transfers between devices  0.86 us (2%)
  between operations  0.74 us (2%)
    all_to_all x1, blocking collectives, shards(): lax.all_to_all(pair.reshape(groups * 2, share // 2, width), DP + ('mp',),...  23.8 us
    ppermute x1, starting transfers between devices, shards(): far = lax.ppermute(second, DP + ('mp',), cross)  4.28 us
    pallas_call x1, Pallas kernels, shards(): pl.pallas_call(local_kernel, out_shape=(wide_rows, wide_rows, jax.ShapeDt...  2.85 us
    pallas_call x1, Pallas kernels, shards(): pl.pallas_call(page_kernel, out_shape=(jax.ShapeDtypeStruct((patches, per...  1.38 us
    unnamed x12, local copies, waits for them, and re-layouts  1.02 us
    pallas_call x1, Pallas kernels, shards(): pl.pallas_call(functools.partial(main_kernel, pages, per_dev), out_shape=...  0.99 us
  transfers between devices with their start and end apart: 3, of which 2 were waited for; matrix products, arithmetic and copies ran while one was open for 0% of the time, Pallas kernels for 11%

profile of v6, /device:TPU:32, one launch (start us, length us, event | category | flops | bytes accessed | tf_op | source)
XLA Modules:
  0.0 37.4 jit_solution(6532618532389109424)
XLA Ops:
  0.6 0.0 copy-start.3
  0.6 0.0 copy-start.2
  0.7 0.0 copy-start.1
  0.7 0.0 copy-start
  0.7 0.0 copy-start.5
  0.7 0.0 copy-start.4
  0.7 0.6 %copy-done.3 = s32[2]{0:T(128)S(1)} copy-done((s32[2]{0:T(128)S(1)}, s32[2]{0:T(128)}, u32[]{:S(2)}) %copy-start.3) | copy-done | bytes 32
  1.3 0.0 copy-done.2
  1.3 0.1 copy-done.1
  1.4 0.3 copy-done
  1.7 0.6 %gather_rows.1 = (bf16[208,128]{1,0:T(8,128)(2,1)S(1)}, bf16[208,128]{1,0:T(8,128)(2,1)S(1)}, bf16[256,128]{1,0:T(8,128)(2,1)S(1)}, bf16[515,2,128]{2,1,0:T(2,128)(2,1)S(1)}, s32[8,256]{1,0:T(8,128)S(1)}) custom-call(s32[8,128]{1,0:T(8,128)S(1)} %place.1.place_ref, s32[2,2,64]{2,1,0:T(2,128)S(1)} %copy-done.2, s32[1,2]{1,0:T(1,128)S(1)} %bitcast.9, ...), custom_call_target="tpu_custom_call" | custom-call | tf_op jit(solution)/shard_map/gather_rows/pallas_call | solution.py:290
  2.3 4.3 %collective-permute-start.1 = (bf16[208,128]{1,0:T(8,128)(2,1)S(1)}, bf16[208,128]{1,0:T(8,128)(2,1)S(1)}, u32[]{:S(2)}, u32[]{:S(2)}) collective-permute-start(bf16[208,128]{1,0:T(8,128)(2,1)S(1)} %get-tuple-element.28), channel_id=1, source_target_pairs={{0,255},{1,254},{2,4},{3,5},{4,2},{5,3},{6,8},{7,9},{8,6},{9,7},{1... | collective-permute-start | bytes 159752 | tf_op jit(solution)/shard_map/ppermute | solution.py:310
  6.6 0.0 collective-permute-start
  6.6 0.0 copy-done.5
  6.6 0.0 copy-done.4
  6.6 2.8 %local_rows.1 = (f32[1030,128]{1,0:T(8,128)S(1)}, f32[1030,128]{1,0:T(8,128)S(1)}, bf16[1030,256]{1,0:T(8,128)(2,1)S(1)}, f32[128,128]{1,0:T(8,128)S(1)}, f32[12...) custom-call(bf16[208,128]{1,0:T(8,128)(2,1)S(1)} %get-tuple-element., ...), custom_call_target="tpu_custom_call" | custom-call | flops 5000000000 | bytes 1000000 | tf_op jit(solution)/shard_map/local_rows/pallas_call | solution.py:319
  9.5 0.7 %collective-permute-done.1.second_ref = bf16[208,128]{1,0:T(8,128)(2,1)S(1)} collective-permute-done((bf16[208,128]{1,0:T(8,128)(2,1)S(1)}, bf16[208,128]{1,0:T(8,128)(2,1)S(1)}, u32[]{:S(2)}, u32[]{:S(2)}) %collective-permute-start.1) | collective-permute-done | bytes 53280 | tf_op jit(solution)/shard_map/ppermute | solution.py:310
  10.2 0.0 collective-permute-done.first_ref
  10.2 1.0 %grads_and_partial.1 = (f32[2,16,128]{2,1,0:T(8,128)S(1)}, bf16[256,256]{1,0:T(8,128)(2,1)S(1)}, bf16[288,128]{1,0:T(8,128)(2,1)S(1)}, bf16[64,16,128]{2,1,0:T(8,128)(2,1)S(1)}) custom-call(bf16[208,128]{1,0:T(8,128)(2,1)S(1)} %get-tuple-element.27.sent_ref, bf16[208,128]{1,0:T(8,128)(2,1)S(1)} %collective-permute-done.first_ref, ...), custom_call_target="tpu_custom_call" | custom-call | tf_op jit(solution)/shard_map/grads_and_partial/pallas_call | solution.py:341
  11.2 0.1 collective-permute-start.2
  11.3 1.4 %page_grads.1 = (f32[515,2,128]{2,1,0:T(2,128)}, f32[2,16,128]{2,1,0:T(8,128)}, f32[64,16,128]{2,1,0:T(8,128)S(1)}) custom-call(bf16[256,256]{1,0:T(8,128)(2,1)S(1)} %get-tuple-element.40.values_ref, bf16[288,128]{1,0:T(8,128)(2,1)S(1)} %get-tuple-element.41.low_ref, bf16[64,16,288]{2,1,0:T(8,128)(2,1)S(1)} %get-tuple-element.42.here_ref, ...), custom_call_target="tpu_custom_call" | custom-call | flops 1000000000 | bytes 1000000 | tf_op jit(solution)/shard_map/page_grads/pallas_call | solution.py:355
  12.7 0.1 collective-permute-done.2.got_ref
  12.9 23.8 %all_to_all.5 = bf16[128,8,128]{2,1,0:T(8,128)(2,1)S(1)} all-to-all(bf16[128,8,128]{2,1,0:T(8,128)(2,1)S(1)} %bitcast.7), channel_id=1, replica_groups={{252,253,236,237,244,245,228,229,248,249,232,233,240,241,224,225,124,12..., dimensions={0} | all-to-all | bytes 524288 | tf_op jit(solution)/shard_map/all_to_all | solution.py:378
  36.7 0.7 %sum_parts.1 = f32[8,128]{1,0:T(8,128)} custom-call(bf16[64,16,128]{2,1,0:T(8,128)(2,1)S(1)} %bitcast.6), custom_call_target="tpu_custom_call" | custom-call | tf_op jit(solution)/shard_map/sum_parts/pallas_call | solution.py:386
  (2 shorter events, 0.1 us)
Async XLA Ops:
  0.6 0.7 %copy-start.3 = (s32[2]{0:T(128)S(1)}, s32[2]{0:T(128)}, u32[]{:S(2)}) copy-start(s32[2]{0:T(128)} %param.11) | copy-start | bytes 28
  0.6 0.7 %copy-start.2 = (s32[2,2,64]{2,1,0:T(2,128)S(1)}, s32[2,2,64]{2,1,0:T(2,128)}, u32[]{:S(2)}) copy-start(s32[2,2,64]{2,1,0:T(2,128)} %idx_ref.1) | copy-start | bytes 3076
  0.7 0.7 %copy-start.1 = (bf16[2,32,128]{2,1,0:T(8,128)(2,1)S(1)}, bf16[2,32,128]{2,1,0:T(8,128)(2,1)}, u32[]{:S(2)}) copy-start(bf16[2,32,128]{2,1,0:T(8,128)(2,1)} %query_ref.1) | copy-start | bytes 49156
  0.7 1.1 %copy-start = (bf16[2,1030,128]{2,0,1:T(2,128)(2,1)S(1)}, bf16[2,1030,128]{2,0,1:T(2,128)(2,1)}, u32[]{:S(2)}) copy-start(bf16[2,1030,128]{2,0,1:T(2,128)(2,1)} %param.8) | copy-start | bytes 1582084
  0.7 6.0 %copy-start.5 = (bf16[2,16,2048]{2,1,0:T(8,128)(2,1)S(1)}, bf16[2,16,2048]{2,1,0:T(8,128)(2,1)}, u32[]{:S(2)}) copy-start(bf16[2,16,2048]{2,1,0:T(8,128)(2,1)} %qhid_ref.1) | copy-start | bytes 393220
  0.7 6.0 %copy-start.4 = (bf16[2,515,2048]{2,0,1:T(2,128)(2,1)S(1)}, bf16[2,515,2048]{2,0,1:T(2,128)(2,1)}, u32[]{:S(2)}) copy-start(bf16[2,515,2048]{2,0,1:T(2,128)(2,1)} %param.6) | copy-start | bytes 12656644
  2.3 7.9 %collective-permute-start.1 = (bf16[208,128]{1,0:T(8,128)(2,1)S(1)}, bf16[208,128]{1,0:T(8,128)(2,1)S(1)}, u32[]{:S(2)}, u32[]{:S(2)}) collective-permute-start(bf16[208,128]{1,0:T(8,128)(2,1)S(1)} %get-tuple-element.28), channel_id=1, source_target_pairs={{0,255},{1,254},{2,4},{3,5},{4,2},{5,3},{6,8},{7,9},{8,6},{9,7},{1... | collective-permute-start | bytes 159752 | tf_op jit(solution)/shard_map/ppermute | solution.py:310
  6.6 3.6 %collective-permute-start = (bf16[208,128]{1,0:T(8,128)(2,1)S(1)}, bf16[208,128]{1,0:T(8,128)(2,1)S(1)}, u32[]{:S(2)}, u32[]{:S(2)}) collective-permute-start(bf16[208,128]{1,0:T(8,128)(2,1)S(1)} %get-tuple-element.27.sent_ref), channel_id=1, source_target_pairs={{0,2},{2,0},{4,6},{6,4},{8,10},{10,8},{12,14},{14,12},{16,18},{18,... | collective-permute-start | bytes 159752 | tf_op jit(solution)/shard_map/ppermute | solution.py:311
  11.2 1.6 %collective-permute-start.2 = (bf16[64,16,128]{2,1,0:T(8,128)(2,1)S(1)}, bf16[64,16,128]{2,1,0:T(8,128)(2,1)S(1)}, u32[]{:S(2)}, u32[]{:S(2)}) collective-permute-start(bf16[64,16,128]{2,1,0:T(8,128)(2,1)S(1)} %get-tuple-element.50), channel_id=1, source_target_pairs={{0,2},{2,0},{1,3},{3,1},{4,6},{6,4},{5,7},{7,5},{8,10},{10,8},{9,1... | collective-permute-start | bytes 786440 | tf_op jit(solution)/shard_map/ppermute | solution.py:354
